TPU v7x, 32 devices: a whole 2x2x4 slice. The times are simulated.
32 devices in a mesh: gz: 4 (over y, core), gy: 8 (over z, x).
Axes of the slice: x: 2, y: 2, z: 4, core: 2. Of those that a mesh axis runs over, the one named last changes fastest.
Arguments:
- image: bfloat16 [32, 16, 1024], P(('gz', 'gy')), may hold values from -8 to 8
- offsets: int32 [32, 2], P(('gz', 'gy')), may hold values from -32 to 32, as said below
- w_stem: bfloat16 [9, 32, 1], replicated, may hold values from -2 to 2
- b_stem: float32 [32], replicated, may hold values from -1.75 to 1.75
- w_skip: bfloat16 [9, 32, 32], replicated, may hold values from -0.375 to 0.375
- b_skip: float32 [32], replicated, may hold values from -1.75 to 1.75
- w_coarse: bfloat16 [27, 64, 32], replicated, may hold values from -0.21875 to 0.21875
- b_coarse: float32 [64], replicated, may hold values from -1.75 to 1.75
- w_lift: bfloat16 [32, 64], replicated, may hold values from -0.75 to 0.75
- b_lift: float32 [32], replicated, may hold values from -1.75 to 1.75
- w_final: bfloat16 [9, 32, 32], replicated, may hold values from -0.375 to 0.375
- b_final: float32 [32], replicated, may hold values from -1.75 to 1.75
- w_head: bfloat16 [3, 32], replicated, may hold values from -1 to 1
- b_head: float32 [3], replicated, may hold values from -3 to 3
Outputs:
- affinity: float32 [3, 32, 16, 1024], P(None, None, 'gy', 'gz')
Inputs may be any that keep to these rules, and one draw needn't show every extreme that they name: offsets[s, 0] and offsets[s, 1] are section s's shifts along y and along x in pixels.
All inputs are finite; a program needn't handle non-finite values.
Results may differ from a plain program's by a relative error of at most 0.0054.
Values may be sent and summed in bfloat16 or wider, within the bound.
No kernel may reach another device: no remote copies, remote signals or barrier semaphores. Data moves between devices by JAX's collectives and lax.ppermute only.
A program may use at most 256 MiB of HBM per device.

v0:
```python
import functools

import jax
import jax.numpy as jnp
from jax import lax
from jax.experimental import pallas as pl
from jax.experimental.pallas import tpu as pltpu
from jax.sharding import PartitionSpec as P

MAXOFF = 32
HALO = 8
SLOTS = 16
HALO_Y = 7
LANES = 128
PAD = MAXOFF + HALO
BF16, F32, I32 = jnp.bfloat16, jnp.float32, jnp.int32
VMEM_BYTES = 58 * 1024 * 1024


def iota(shape, dim):
    return lax.broadcasted_iota(I32, shape, dim)


def dot(a, b):
    return jnp.dot(a, b, preferred_element_type=F32)


def dot_tn(a, b):
    return lax.dot_general(a, b, (((0,), (0,)), ((), ())), preferred_element_type=F32)


def dot_nt(a, b):
    return lax.dot_general(a, b, (((1,), (1,)), ((), ())), preferred_element_type=F32)


def relu(x):
    return jnp.maximum(x, 0.0)


def round_up(n, m):
    return -(-n // m) * m


def divisor(count, most):
    return max(d for d in range(1, count + 1) if count % d == 0 and d <= max(most, 1))


def send_kernel(parts_gz, parts_gy, brick_y, brick_x, off_ref, image_ref, send_ref, tall_ref):
    full_y, full_x = image_ref.shape[1:]
    blocks = full_x // 8 + 2
    rows = round_up(blocks, 8)
    mine = brick_x // 8 + 2
    off_y, off_x = off_ref[0, 0], off_ref[0, 1]
    tall_ref[...] = jnp.zeros_like(tall_ref)
    tall_ref[PAD : PAD + full_x, 0:full_y] = image_ref[0].astype(F32).T
    lane, block = iota((rows, LANES), 1), iota((rows, LANES), 0)
    in_section = (block >= 1) & (block < blocks - 1)
    halves = full_y // SLOTS
    packed = [jnp.zeros((rows, LANES), F32) for _ in range(halves)]
    for i in range(8):
        column = tall_ref[pl.ds(PAD - HALO + i - off_x, rows, stride=8), :]
        for h in range(halves):
            turn = lax.rem(off_y + (16 * i - 16 * h + 2 * LANES), LANES)
            turned = pltpu.roll(column, turn, axis=1)
            packed[h] = jnp.where(((lane >> 4) == i) & in_section, turned, packed[h])
    slot = lane & 15
    for gy in range(parts_gy):
        start = brick_y * gy - HALO_Y
        window = jnp.zeros((rows, LANES), F32)
        for h in range(halves):
            shift = start - 16 * h
            if -16 < shift < 16:
                turned = pltpu.roll(packed[h], (-shift) % LANES, axis=1)
                inside = (slot + shift >= 0) & (slot + shift < 16)
                window = jnp.where(inside, turned, window)
        for gz in range(parts_gz):
            first = gz * (brick_x // 8)
            send_ref[gz * parts_gy + gy] = window[first : first + mine].astype(BF16)


def make_windows(image, offsets, parts_gz, parts_gy):
    full_y, full_x = image.shape[1:]
    brick_y, brick_x = full_y // parts_gy, full_x // parts_gz
    rows = round_up(full_x // 8 + 2, 8)
    tall = round_up(PAD - HALO + 7 + MAXOFF + 8 * (rows - 1) + 1, 8)
    return pl.pallas_call(
        functools.partial(send_kernel, parts_gz, parts_gy, brick_y, brick_x),
        out_shape=jax.ShapeDtypeStruct((parts_gz * parts_gy, brick_x // 8 + 2, LANES), BF16),
        in_specs=[
            pl.BlockSpec(memory_space=pltpu.SMEM),
            pl.BlockSpec(memory_space=pltpu.VMEM),
        ],
        out_specs=pl.BlockSpec(memory_space=pltpu.VMEM),
        scratch_shapes=[pltpu.VMEM((tall, LANES), F32)],
    )(offsets, image)


def stem_row(s):
    return jnp.where(s < 8, s + 2, jnp.where(s < 12, s - 8, s - 4))


def within(y, full_y):
    return (y >= 0) & (y < full_y)


def prep_kernel(
    brick_y,
    full_y,
    pos_ref,
    w_stem,
    w_skip,
    w_coarse,
    w_lift,
    w_final,
    w_head,
    b4,
    b_coarse,
    ws,
    wa,
    wb,
    wc,
    wl,
    wf,
    wh,
    bias,
):
    y0 = pos_ref[1] * brick_y
    zero = jnp.zeros((32, 256), F32)

    def tiles(count, width):
        return jnp.where((iota((count, width), 1) & (count - 1)) == iota((count, width), 0), 1.0, 0.0)

    t512_f, t256_f, t64_f = tiles(32, 512), tiles(32, 256), tiles(64, 256)
    t512, t256, t64 = t512_f.astype(BF16), t256_f.astype(BF16), t64_f.astype(BF16)

    def spread(row, table):
        return jnp.dot(row, table, precision=lax.Precision.HIGHEST, preferred_element_type=F32)

    lane = iota((1, 512), 1)
    t_of = stem_row(lane >> 5)
    stem_ok = within(y0 - 5 + t_of, full_y)
    rep = dot(w_stem[...], t512)
    lane16 = iota((16, 512), 1)
    t16 = stem_row(lane16 >> 5)
    tap16 = iota((16, 512), 0) - t16 - 1
    ok16 = within(y0 - 5 + t16, full_y)
    ws[...] = jnp.zeros_like(ws)
    for dx in range(3):
        block = jnp.zeros((16, 512), F32)
        for a in range(3):
            block = jnp.where((tap16 == a) & ok16, rep[3 * a + dx : 3 * a + dx + 1], block)
        ws[112 + 16 * dx : 128 + 16 * dx] = block.astype(BF16)
    bias[...] = jnp.zeros_like(bias)
    bias[0:1] = jnp.where(stem_ok, spread(b4[0:1], t512_f), 0.0)

    lane = iota((32, 256), 1)
    half, quarter = lane >> 7, (lane >> 5) & 3
    row_a = 2 + 2 * quarter + half
    ok_a = (quarter < 3) & within(y0 - 4 + row_a, full_y)
    row_a = jnp.where(ok_a, row_a, -99)
    xpar = quarter >> 1
    row_b = 8 * (quarter & 1) + half
    ok_b = within(y0 - 4 + row_b, full_y)
    row_b = jnp.where(ok_b, row_b, -99)
    reps = [dot_tn(w_skip[tap], t256) for tap in range(9)]
    for dx in range(3):
        for i in range(8):
            block = zero
            for a in range(3):
                block = jnp.where(row_a == 2 + i - a, reps[3 * a + dx], block)
            wa[256 * dx + 32 * i : 256 * dx + 32 * i + 32] = block.astype(BF16)
    for j in range(4):
        for i in range(8):
            t = i if i < 4 else i + 4
            block = zero
            for a in range(3):
                for p in range(2):
                    if 0 <= j - p < 3:
                        block = jnp.where(
                            (row_b == t - a) & (xpar == p), reps[3 * a + j - p], block
                        )
            wb[256 * j + 32 * i : 256 * j + 32 * i + 32] = block.astype(BF16)
    b_skip = spread(b4[1:2], t256_f)
    bias[1:2, 0:256] = jnp.where(ok_a[0:1], b_skip, 0.0)
    bias[2:3, 0:256] = jnp.where(ok_b[0:1], b_skip, 0.0)

    slots = []
    for c in range(3):
        slots += [(1, c), (2, c), (3, c), ((None, 0), (0, 2), (4, 2))[c]]
    slots += [(0, 0), (4, 0), (0, 1), (4, 1)]
    q_of = lane >> 6
    for dx in range(3):
        reps = [dot_tn(w_coarse[3 * ca + dx], t64) for ca in range(9)]
        for i, (p, c) in enumerate(slots):
            block = zero
            if p is not None:
                for a in range(3):
                    block = jnp.where(q_of == p - a, reps[3 * c + a], block)
            wc[512 * dx + 32 * i : 512 * dx + 32 * i + 32] = block.astype(BF16)
    bias[3:4, 0:256] = spread(b_coarse[...], t64_f)

    lane64 = iota((64, 256), 1)
    quarter64 = (lane64 >> 5) & 3
    ok64 = within(y0 - 2 + 2 * quarter64 + (lane64 >> 7), full_y)
    rep = dot_tn(w_lift[...], t256)
    for q in range(3):
        wl[64 * q : 64 * q + 64] = jnp.where((quarter64 == q) & ok64, rep, 0.0).astype(BF16)
    wl[192:256] = jnp.zeros((64, 256), BF16)
    bias[4:5, 0:256] = jnp.where(ok_a[0:1], spread(b4[2:3], t256_f), 0.0)

    xi_of, f_of = lane >> 6, (lane >> 5) & 1
    reps = [dot_tn(w_final[tap], t256) for tap in range(9)]
    for j in range(6):
        for i in range(8):
            row = 2 + 2 * (i & 3) + (i >> 2)
            block = zero
            if (i & 3) < 3:
                for a in range(3):
                    for dx in range(3):
                        if 0 <= row - 3 - a < 2 and 0 <= j - dx < 4:
                            block = jnp.where(
                                (f_of == row - 3 - a) & (xi_of == j - dx), reps[3 * a + dx], block
                            )
            wf[256 * j + 32 * i : 256 * j + 32 * i + 32] = block.astype(BF16)
    bias[5:6, 0:256] = spread(b4[3:4], t256_f)

    row = iota((32, 256), 0)
    rep = dot(w_head[...], t256)
    block = zero
    for o in range(3):
        here = ((row >> 3) == xi_of) & ((row & 7) == 2 * o + f_of)
        block = jnp.where(here, rep[o : o + 1], block)
    wh[...] = block.astype(BF16)


def prepare(pos, brick_y, full_y, w_stem, w_skip, w_coarse, w_lift, w_final, w_head, b4, b_coarse):
    shapes = [(272, 512), (768, 256), (1024, 256), (1536, 256), (256, 256), (1536, 256), (32, 256)]
    vmem = pl.BlockSpec(memory_space=pltpu.VMEM)
    return pl.pallas_call(
        functools.partial(prep_kernel, brick_y, full_y),
        out_shape=[jax.ShapeDtypeStruct(s, BF16) for s in shapes]
        + [jax.ShapeDtypeStruct((8, 512), F32)],
        in_specs=[pl.BlockSpec(memory_space=pltpu.SMEM)] + [vmem] * 8,
        out_specs=[vmem] * 8,
        cost_estimate=pl.CostEstimate(
            flops=100_000_000, bytes_accessed=4_000_000, transcendentals=0
        ),
        compiler_params=pltpu.CompilerParams(vmem_limit_bytes=VMEM_BYTES),
    )(pos, w_stem, w_skip, w_coarse, w_lift, w_final, w_head, b4, b_coarse)


def brick_kernel(
    parts_gz,
    cols,
    steps,
    pos_ref,
    b_head,
    r_ref,
    ws,
    wa,
    wb,
    wc,
    wl,
    wf,
    wh,
    bias,
    out_ref,
    tmp,
    rin,
    stem,
    skip,
    pooled,
    fin,
):
    nz, have = r_ref.shape[0:2]
    pitch = tmp.shape[0] // nz
    blocks = cols // 8 + 2
    step = 0 if steps == 1 else pl.program_id(0)
    leftmost = (pos_ref[0] == 0) & (step == 0)
    rightmost = (pos_ref[0] == parts_gz - 1) & (step == steps - 1)

    for z in range(nz):
        tmp[z * pitch : z * pitch + have] = r_ref[z].astype(F32)
    for b in range(blocks):
        rin[b] = tmp[pl.ds(step * (cols // 8) + b, nz, stride=pitch), :].astype(BF16)

    b_stem = bias[0:1, :]

    def stem_put(acc, first, i):
        out = relu(acc + b_stem).astype(BF16)
        for b in range(acc.shape[0] // nz):
            stem[4 * (first + b) + (i >> 1), i & 1] = out[b * nz : b * nz + nz]

    def stem_mid(i, carry):
        start = pl.multiple_of(128 - 16 * i, 16)
        weight = ws[pl.ds(start, LANES), :]
        stem_put(dot(rin[...].reshape(blocks * nz, LANES), weight), 0, i)
        return carry

    lax.fori_loop(1, 7, stem_mid, 0)
    pair = jnp.concatenate([rin[0 : blocks - 1], rin[1:blocks]], axis=-1)
    pair = pair.reshape((blocks - 1) * nz, 2 * LANES)
    stem_put(dot(pair, ws[0:256]), 1, 0)
    stem_put(dot(pair, ws[16:272]), 0, 7)

    @pl.when(leftmost)
    def _():
        stem[0:4] = jnp.zeros((4,) + stem.shape[1:], BF16)

    @pl.when(rightmost)
    def _():
        stem[4 * blocks - 4 : 4 * blocks] = jnp.zeros((4,) + stem.shape[1:], BF16)

    pairs = cols // 2 + 4
    mc = divisor(pairs, 512 // nz)
    m_rows = mc * nz

    def skip_step(i, carry):
        m0 = i * mc

        def taken(u, half):
            part = stem[pl.ds(m0 + u // 2, mc), u % 2, :, 256 * half : 256 * half + 256]
            return part.reshape(m_rows, 256)

        top = None
        for p in range(2):
            acc = dot(taken(3 + p, 0), wa[0:256])
            acc += dot(taken(4 + p, 0), wa[256:512])
            acc += dot(taken(5 + p, 0), wa[512:768])
            acc = relu(acc + bias[1:2, 0:256])
            skip[pl.ds(m0, mc), p] = acc.astype(BF16).reshape(mc, nz, 256)
            best = jnp.maximum(acc[:, 0:128], acc[:, 128:256])
            top = best if top is None else jnp.maximum(top, best)
        acc = dot(taken(3, 1), wb[0:256])
        for j in range(1, 4):
            acc += dot(taken(3 + j, 1), wb[256 * j : 256 * j + 256])
        best = jnp.maximum(acc[:, 0:128], acc[:, 128:256])
        best = jnp.maximum(best, pltpu.roll(best, 64, axis=1))
        ends = relu(best + bias[2:3, 0:128])
        z_of = iota((mc, nz, LANES), 1).reshape(m_rows, LANES)
        lane = iota((m_rows, LANES), 1)
        bottom, summit = z_of == 0, z_of == nz - 1

        def below(x):
            return jnp.where(bottom, 0.0, pltpu.roll(x, 1, axis=0))

        def above(x):
            return jnp.where(summit, 0.0, pltpu.roll(x, m_rows - 1, axis=0))

        ends_above = above(ends)
        parts = (
            below(top),
            jnp.where(lane < 96, top, pltpu.roll(ends_above, 32, axis=1)),
            jnp.where(lane < 96, above(top), ends_above),
            jnp.where(lane < 64, below(ends), ends),
        )
        for k in range(4):
            pooled[pl.ds(m0, mc), :, 128 * k : 128 * k + 128] = (
                parts[k].astype(BF16).reshape(mc, nz, LANES)
            )
        return carry

    lax.fori_loop(0, pairs // mc, skip_step, 0)

    @pl.when(leftmost)
    def _():
        pooled[0:2] = jnp.zeros((2,) + pooled.shape[1:], BF16)

    @pl.when(rightmost)
    def _():
        pooled[pairs - 2 : pairs] = jnp.zeros((2,) + pooled.shape[1:], BF16)

    count = cols // 2 + 2
    nc = divisor(count, 512 // nz)
    n_rows = nc * nz

    def coarse_step(i, carry):
        n0 = i * nc
        acc = dot(pooled[pl.ds(n0, nc)].reshape(n_rows, 512), wc[0:512])
        acc += dot(pooled[pl.ds(n0 + 1, nc)].reshape(n_rows, 512), wc[512:1024])
        acc += dot(pooled[pl.ds(n0 + 2, nc)].reshape(n_rows, 512), wc[1024:1536])
        coarse = relu(acc + bias[3:4, 0:256]).astype(BF16)
        lifted = dot(coarse, wl[...])
        for p in range(2):
            base = skip[pl.ds(n0 + 1, nc), p].reshape(n_rows, 256).astype(F32)
            out = relu(base + lifted + bias[4:5, 0:256]).astype(BF16)
            for k in range(nc):
                n = n0 + k
                stem[n >> 1, n & 1, :, 256 * p : 256 * p + 256] = out[k * nz : k * nz + nz]
        return carry

    lax.fori_loop(0, count // nc, coarse_step, 0)

    @pl.when(leftmost)
    def _():
        stem[0, 0] = jnp.zeros(stem.shape[2:], BF16)

    @pl.when(rightmost)
    def _():
        stem[cols // 4, 1] = jnp.zeros(stem.shape[2:], BF16)

    quads = cols // 4
    qc = divisor(quads, 512 // nz)
    q_rows = qc * nz

    def final_step(i, carry):
        q0 = i * qc
        acc = jnp.zeros((q_rows, 256), F32)
        for j in range(6):
            k = (1 + j) % 4
            half = 256 * (k % 2)
            part = stem[pl.ds(q0 + (1 + j) // 4, qc), k // 2, :, half : half + 256]
            acc += dot(part.reshape(q_rows, 256), wf[256 * j : 256 * j + 256])
        out = relu(acc + bias[5:6, 0:256])
        for k in range(2):
            fin[k, pl.ds(pl.multiple_of(q0 * nz, 8), q_rows), :] = out[:, 128 * k : 128 * k + 128]
        return carry

    lax.fori_loop(0, quads // qc, final_step, 0)

    together = LANES // quads
    groups = nz // together
    lines = []
    for g in range(groups):
        sides = []
        for side in range(2):
            rows = [
                fin[side, pl.ds(g * together + k, quads, stride=nz), :] for k in range(together)
            ]
            sides.append(jnp.concatenate(rows, axis=0).astype(BF16))
        h = dot_nt(wh[...], jnp.concatenate(sides, axis=1))
        lines.append(jnp.concatenate([h[8 * xi : 8 * xi + 8] for xi in range(4)], axis=1))
    table = jnp.concatenate(lines, axis=0)
    size = together * cols
    row = iota((512, size), 0)
    order = jnp.where(iota((512, size), 1) == 4 * (row & 127) + (row >> 7), 1.0, 0.0).astype(BF16)
    high = table.astype(BF16)
    rest = table - high.astype(F32)
    middle = rest.astype(BF16)
    low = (rest - middle.astype(F32)).astype(BF16)
    result = dot(high, order) + (dot(middle, order) + dot(low, order))
    for g in range(groups):
        for k in range(together):
            for o in range(3):
                out_ref[o, g * together + k] = (
                    result[8 * g + 2 * o : 8 * g + 2 * o + 2, k * cols : k * cols + cols]
                    + b_head[o]
                )


def brick(pos, b_head, received, weights, parts_gz, brick_y, brick_x):
    nz, have = received.shape[0:2]
    cols = brick_x
    while cols * nz > 16384 and cols % 256 == 0:
        cols //= 2
    steps = brick_x // cols
    vmem = pl.BlockSpec(memory_space=pltpu.VMEM)
    smem = pl.BlockSpec(memory_space=pltpu.SMEM)
    return pl.pallas_call(
        functools.partial(brick_kernel, parts_gz, cols, steps),
        grid=(steps,),
        out_shape=jax.ShapeDtypeStruct((3, nz, brick_y, brick_x), F32),
        in_specs=[smem, smem] + [vmem] * 9,
        out_specs=pl.BlockSpec((3, nz, brick_y, cols), lambda i: (0, 0, 0, i)),
        scratch_shapes=[
            pltpu.VMEM((nz * round_up(have, 8), LANES), F32),
            pltpu.VMEM((cols // 8 + 2, nz, LANES), BF16),
            pltpu.VMEM((cols // 2 + 8, 2, nz, 512), BF16),
            pltpu.VMEM((cols // 2 + 4, 2, nz, 256), BF16),
            pltpu.VMEM((cols // 2 + 4, nz, 512), BF16),
            pltpu.VMEM((2, cols // 4 * nz, LANES), F32),
        ],
        cost_estimate=pl.CostEstimate(
            flops=20_000_000_000, bytes_accessed=4_000_000, transcendentals=0
        ),
        compiler_params=pltpu.CompilerParams(vmem_limit_bytes=VMEM_BYTES),
    )(pos, b_head, received, *weights)


def local(
    image,
    offsets,
    w_stem,
    b_stem,
    w_skip,
    b_skip,
    w_coarse,
    b_coarse,
    w_lift,
    b_lift,
    w_final,
    b_final,
    w_head,
    b_head,
):
    parts_gz, parts_gy = lax.axis_size("gz"), lax.axis_size("gy")
    full_y, full_x = image.shape[1:]
    brick_y, brick_x = full_y // parts_gy, full_x // parts_gz
    assert image.shape[0] == 1 and brick_y == 2
    pos = jnp.stack([lax.axis_index("gz"), lax.axis_index("gy")]).astype(I32)
    windows = make_windows(image, offsets, parts_gz, parts_gy)
    received = lax.all_to_all(windows, ("gz", "gy"), 0, 0, tiled=True)
    b4 = jnp.stack([b_stem, b_skip, b_lift, b_final])
    weights = prepare(
        pos,
        brick_y,
        full_y,
        w_stem.reshape(w_stem.shape[0:2]),
        w_skip,
        w_coarse,
        w_lift,
        w_final,
        w_head,
        b4,
        b_coarse[None],
    )
    return brick(pos, b_head, received, weights, parts_gz, brick_y, brick_x)


def solution(mesh):
    split = P(("gz", "gy"))
    return jax.shard_map(
        local,
        mesh=mesh,
        in_specs=(split, split) + (P(),) * 12,
        out_specs=P(None, None, "gy", "gz"),
        check_vma=False,
    )
```

profile of v0, /device:TPU:0, one launch (start us, length us, event | category | flops | bytes accessed | tf_op | source)
XLA Modules:
  0.0 48.4 jit_solution(11684879493836282131)
XLA Ops:
  0.0 2.0 %shard_map.136 = bf16[32,34,128]{2,1,0:T(8,128)(2,1)} custom-call(s32[1,2]{1,0:T(1,128)} %off_ref.1, bf16[1,16,1024]{2,1,0:T(8,128)(2,1)} %image_ref.1), custom_call_target="tpu_custom_call" | custom-call | tf_op jit(solution)/shard_map/pallas_call | solution.py:86
  2.0 0.0 copy-start.1
  2.0 7.3 %all-to-all-start = ((bf16[32,34,128]{2,1,0:T(8,128)(2,1)}), bf16[32,34,128]{2,1,0:T(8,128)(2,1)S(1)}, u32[]{:S(2)}, u32[]{:S(2)}) async-start(bf16[32,34,128]{2,1,0:T(8,128)(2,1)} %shard_map.136), calls=%async_computation | async-start | bytes 655360 | tf_op jit(solution)/shard_map/all_to_all | solution.py:502
  9.3 0.0 copy-done.1
  9.3 0.0 copy-start.5
  9.3 1.0 %copy.15.w_coarse = bf16[27,64,32]{2,1,0:T(8,128)(2,1)} copy(bf16[27,64,32]{1,2,0:T(8,128)(2,1)S(1)} %copy-done.1) | data formatting | bytes 221184 | tf_op args[6]
  10.3 0.6 %pad_add_fusion.pos_ref = s32[2]{0:T(128)} fusion(s32[1]{0:T(128)} %bitcast.1, s32[1]{0:T(128)} %bitcast), kind=kLoop, calls=%fused_computation.1 | loop fusion | flops 2 | bytes 16 | tf_op jit(solution)/shard_map/stack | solution.py:500
  10.9 0.0 copy-start.2
  10.9 0.0 copy-start.3
  10.9 0.0 copy-start.4
  10.9 0.0 copy-done.5
  10.9 0.6 %copy-done.2 = f32[32]{0:T(128)S(1)} copy-done((f32[32]{0:T(128)S(1)}, f32[32]{0:T(128)}, u32[]{:S(2)}) %copy-start.2) | copy-done | bytes 152
  11.6 0.0 copy-done.3
  11.6 0.0 copy-done.4
  11.6 0.6 %pad_maximum_fusion.b4 = f32[4,32]{1,0:T(4,128)} fusion(f32[1,32]{1,0:T(1,128)S(1)} %bitcast.10, f32[1,32]{1,0:T(1,128)S(1)} %bitcast.11, f32[1,32]{1,0:T(1,128)S(1)} %bitcast.12, f32[1,32]{1,0:T(1,128)S(1)} %bitcast.13), kind=kLoop, calls=%fused_computation | loop fusion | flops 384 | bytes 1024 | tf_op jit(solution)/shard_map/stack | solution.py:503
  12.2 3.5 %shard_map.137 = (bf16[272,512]{1,0:T(8,128)(2,1)}, bf16[768,256]{1,0:T(8,128)(2,1)}, bf16[1024,256]{1,0:T(8,128)(2,1)}, bf16[1536,256]{1,0:T(8,128)(2,1)}, bf16...) custom-call(s32[2]{0:T(128)} %pad_add_fusion.pos_ref, ...), custom_call_target="tpu_custom_call" | custom-call | flops 100000000 | bytes 4000000 | tf_op jit(solution)/shard_map/pallas_call | solution.py:239
  15.7 5.7 %all-to-all-done.r_ref = bf16[32,34,128]{2,1,0:T(8,128)(2,1)S(1)} async-done(((bf16[32,34,128]{2,1,0:T(8,128)(2,1)}), bf16[32,34,128]{2,1,0:T(8,128)(2,1)S(1)}, u32[]{:S(2)}, u32[]{:S(2)}) %all-to-all-start) | async-done | bytes 278560 | tf_op jit(solution)/shard_map/all_to_all | solution.py:502
  21.5 0.0 copy-start
  21.5 0.7 %copy-done = bf16[32,34,128]{2,1,0:T(8,128)(2,1)} copy-done((bf16[32,34,128]{2,1,0:T(8,128)(2,1)}, bf16[32,34,128]{2,1,0:T(8,128)(2,1)S(1)}, u32[]{:S(2)}) %copy-start) | copy-done | bytes 278552
  22.2 26.2 %shard_map.138 = f32[3,32,2,256]{3,2,1,0:T(2,128)} custom-call(s32[2]{0:T(128)} %pad_add_fusion.pos_ref, f32[3]{0:T(128)} %b_head.1, bf16[32,34,128]{2,1,0:T(8,128)(2,1)} %copy-done, bf16[272,512]{1,0:T(8,128)(2,1)} %get-tuple-element.13.ws, bf16[768,256]{1,0:T(8,128)(2,1)} %get-tuple-element.14.wa, bf16[1024,256]{1,0:T(8,128)(2,1)} %get-tuple-element.15.wb, ...), custom_call_target="tpu_custom_call" | custom-call | flops 20000000000 | bytes 4000000 | tf_op jit(solution)/shard_map/pallas_call | solution.py:459
Async XLA Ops:
  2.0 7.3 %copy-start.1 = (bf16[27,64,32]{1,2,0:T(8,128)(2,1)S(1)}, bf16[27,64,32]{1,2,0:T(8,128)(2,1)}, u32[]{:S(2)}) copy-start(bf16[27,64,32]{1,2,0:T(8,128)(2,1)} %param.20) | copy-start | bytes 331780
  2.0 19.4 %all-to-all-start = ((bf16[32,34,128]{2,1,0:T(8,128)(2,1)}), bf16[32,34,128]{2,1,0:T(8,128)(2,1)S(1)}, u32[]{:S(2)}, u32[]{:S(2)}) async-start(bf16[32,34,128]{2,1,0:T(8,128)(2,1)} %shard_map.136), calls=%async_computation | async-start | bytes 655360 | tf_op jit(solution)/shard_map/all_to_all | solution.py:502
  9.3 1.6 %copy-start.5 = (f32[32]{0:T(128)S(1)}, f32[32]{0:T(128)}, u32[]{:S(2)}) copy-start(f32[32]{0:T(128)} %param.17) | copy-start | bytes 388
  10.9 0.7 %copy-start.2 = (f32[32]{0:T(128)S(1)}, f32[32]{0:T(128)}, u32[]{:S(2)}) copy-start(f32[32]{0:T(128)} %param.25) | copy-start | bytes 388
  10.9 0.7 %copy-start.3 = (f32[32]{0:T(128)S(1)}, f32[32]{0:T(128)}, u32[]{:S(2)}) copy-start(f32[32]{0:T(128)} %param.23) | copy-start | bytes 388
  10.9 0.7 %copy-start.4 = (f32[32]{0:T(128)S(1)}, f32[32]{0:T(128)}, u32[]{:S(2)}) copy-start(f32[32]{0:T(128)} %param.19) | copy-start | bytes 388
  21.5 0.7 %copy-start = (bf16[32,34,128]{2,1,0:T(8,128)(2,1)}, bf16[32,34,128]{2,1,0:T(8,128)(2,1)S(1)}, u32[]{:S(2)}) copy-start(bf16[32,34,128]{2,1,0:T(8,128)(2,1)S(1)} %all-to-all-done.r_ref) | copy-start | bytes 835588
where the time goes:
time: 48.7 us; the launch traced here: 48.4 us
  Pallas kernels  31.8 us (65%)
  starting transfers between devices  7.3 us (15%)
  waiting for transfers between devices  5.73 us (12%)
  local copies, waits for them, and re-layouts  2.38 us (5%)
  other arithmetic  1.18 us (2%)
    pallas_call x1, Pallas kernels, brick(): pl.pallas_call(functools.partial(brick_kernel, parts_gz, cols, steps), gr...  26.2 us
    all_to_all x1, starting transfers between devices, local(): received = lax.all_to_all(windows, ('gz', 'gy'), 0, 0, tiled=True)  7.3 us
    all_to_all x1, waiting for transfers between devices, local(): received = lax.all_to_all(windows, ('gz', 'gy'), 0, 0, tiled=True)  5.73 us
    pallas_call x1, Pallas kernels, prepare(): pl.pallas_call(functools.partial(prep_kernel, brick_y, full_y), out_shape...  3.55 us
    unnamed x13, local copies, waits for them, and re-layouts  2.38 us
    pallas_call x1, Pallas kernels, make_windows(): pl.pallas_call(functools.partial(send_kernel, parts_gz, parts_gy, brick_y...  2.01 us
  transfers between devices with their start and end apart: 1, of which 1 were waited for; matrix products, arithmetic and copies ran while one was open for 4% of the time, Pallas kernels for 7%

commit v1 on v0

--- a/solution.py
+++ b/solution.py
@@ -1,4 +1,5 @@
 import functools
+import math
 
 import jax
 import jax.numpy as jnp
@@ -14,7 +15,7 @@
 LANES = 128
 PAD = MAXOFF + HALO
 BF16, F32, I32 = jnp.bfloat16, jnp.float32, jnp.int32
-VMEM_BYTES = 58 * 1024 * 1024
+MIB = 1024 * 1024
 
 
 def iota(shape, dim):
@@ -95,8 +96,27 @@
     )(offsets, image)
 
 
+ENDS = (0, 1, 10, 11, 2, 3, 8, 9)
+
+
+SIZES = {"a": 768, "b": 1024, "c": 1536, "l": 256, "f": 1536, "h": 32, "s": 272, "t": 272, "v": 96}
+STARTS = dict(zip(SIZES, [sum(list(SIZES.values())[:k]) for k in range(len(SIZES))]))
+WEIGHT_ROWS = sum(SIZES.values())
+
+
+def parts_of(ref):
+    return [ref.at[STARTS[k] : STARTS[k] + SIZES[k]] for k in SIZES]
+
+
+def in_three(x):
+    high = x.astype(BF16)
+    rest = x - high.astype(F32)
+    middle = rest.astype(BF16)
+    return high, middle, (rest - middle.astype(F32)).astype(BF16)
+
+
 def stem_row(s):
-    return jnp.where(s < 8, s + 2, jnp.where(s < 12, s - 8, s - 4))
+    return jnp.where(s < 8, s + 2, jnp.where(s < 10, s - 8, s))
 
 
 def within(y, full_y):
@@ -107,6 +127,7 @@
     brick_y,
     full_y,
     pos_ref,
+    b_head,
     w_stem,
     w_skip,
     w_coarse,
@@ -115,43 +136,41 @@
     w_head,
     b4,
     b_coarse,
-    ws,
-    wa,
-    wb,
-    wc,
-    wl,
-    wf,
-    wh,
+    packed,
     bias,
 ):
+    wa, wb, wc, wl, wf, wh, ws, wt, wv = parts_of(packed)
     y0 = pos_ref[1] * brick_y
     zero = jnp.zeros((32, 256), F32)
 
     def tiles(count, width):
         return jnp.where((iota((count, width), 1) & (count - 1)) == iota((count, width), 0), 1.0, 0.0)
 
-    t512_f, t256_f, t64_f = tiles(32, 512), tiles(32, 256), tiles(64, 256)
-    t512, t256, t64 = t512_f.astype(BF16), t256_f.astype(BF16), t64_f.astype(BF16)
+    t384_f, t256_f, t64_f = tiles(32, 384), tiles(32, 256), tiles(64, 256)
+    t384, t256, t64 = t384_f.astype(BF16), t256_f.astype(BF16), t64_f.astype(BF16)
 
     def spread(row, table):
         return jnp.dot(row, table, precision=lax.Precision.HIGHEST, preferred_element_type=F32)
 
-    lane = iota((1, 512), 1)
+    lane = iota((1, 384), 1)
     t_of = stem_row(lane >> 5)
     stem_ok = within(y0 - 5 + t_of, full_y)
-    rep = dot(w_stem[...], t512)
-    lane16 = iota((16, 512), 1)
+    rep = dot(w_stem[...], t384)
+    lane16 = iota((16, 384), 1)
     t16 = stem_row(lane16 >> 5)
-    tap16 = iota((16, 512), 0) - t16 - 1
+    tap16 = iota((16, 384), 0) - t16 - 1
     ok16 = within(y0 - 5 + t16, full_y)
-    ws[...] = jnp.zeros_like(ws)
+    ws[...] = jnp.zeros((272, 256), BF16)
+    wt[...] = jnp.zeros((272, 256), BF16)
     for dx in range(3):
-        block = jnp.zeros((16, 512), F32)
+        block = jnp.zeros((16, 384), F32)
         for a in range(3):
             block = jnp.where((tap16 == a) & ok16, rep[3 * a + dx : 3 * a + dx + 1], block)
-        ws[112 + 16 * dx : 128 + 16 * dx] = block.astype(BF16)
+        block = block.astype(BF16)
+        ws[112 + 16 * dx : 128 + 16 * dx] = block[:, 0:256]
+        wt[112 + 16 * dx : 128 + 16 * dx, 0:128] = block[:, 256:384]
     bias[...] = jnp.zeros_like(bias)
-    bias[0:1] = jnp.where(stem_ok, spread(b4[0:1], t512_f), 0.0)
+    bias[0:1, 0:384] = jnp.where(stem_ok, spread(b4[0:1], t384_f), 0.0)
 
     lane = iota((32, 256), 1)
     half, quarter = lane >> 7, (lane >> 5) & 3
@@ -171,7 +190,7 @@
             wa[256 * dx + 32 * i : 256 * dx + 32 * i + 32] = block.astype(BF16)
     for j in range(4):
         for i in range(8):
-            t = i if i < 4 else i + 4
+            t = ENDS[i]
             block = zero
             for a in range(3):
                 for p in range(2):
@@ -231,22 +250,26 @@
         here = ((row >> 3) == xi_of) & ((row & 7) == 2 * o + f_of)
         block = jnp.where(here, rep[o : o + 1], block)
     wh[...] = block.astype(BF16)
-
-
-def prepare(pos, brick_y, full_y, w_stem, w_skip, w_coarse, w_lift, w_final, w_head, b4, b_coarse):
-    shapes = [(272, 512), (768, 256), (1024, 256), (1536, 256), (256, 256), (1536, 256), (32, 256)]
+    kind = iota((8, 512), 0)
+    bias[8:16] = jnp.where(kind < 2, b_head[0], jnp.where(kind < 4, b_head[1], b_head[2]))
+    for k, term in enumerate(in_three(bias[...])):
+        wv[32 * k : 32 * k + 16] = term[:, 0:256]
+        wv[32 * k + 16 : 32 * k + 32] = term[:, 256:512]
+
+
+def prepare(pos, b_head, brick_y, full_y, w_stem, w_skip, w_coarse, w_lift, w_final, w_head, b4, b_coarse):
     vmem = pl.BlockSpec(memory_space=pltpu.VMEM)
     return pl.pallas_call(
         functools.partial(prep_kernel, brick_y, full_y),
-        out_shape=[jax.ShapeDtypeStruct(s, BF16) for s in shapes]
-        + [jax.ShapeDtypeStruct((8, 512), F32)],
-        in_specs=[pl.BlockSpec(memory_space=pltpu.SMEM)] + [vmem] * 8,
-        out_specs=[vmem] * 8,
+        out_shape=jax.ShapeDtypeStruct((WEIGHT_ROWS, 256), BF16),
+        in_specs=[pl.BlockSpec(memory_space=pltpu.SMEM)] * 2 + [vmem] * 8,
+        out_specs=vmem,
+        scratch_shapes=[pltpu.VMEM((16, 512), F32)],
         cost_estimate=pl.CostEstimate(
             flops=100_000_000, bytes_accessed=4_000_000, transcendentals=0
         ),
-        compiler_params=pltpu.CompilerParams(vmem_limit_bytes=VMEM_BYTES),
-    )(pos, w_stem, w_skip, w_coarse, w_lift, w_final, w_head, b4, b_coarse)
+        compiler_params=pltpu.CompilerParams(vmem_limit_bytes=12 * MIB),
+    )(pos, b_head, w_stem, w_skip, w_coarse, w_lift, w_final, w_head, b4, b_coarse)
 
 
 def brick_kernel(
@@ -254,17 +277,10 @@
     cols,
     steps,
     pos_ref,
-    b_head,
     r_ref,
-    ws,
-    wa,
-    wb,
-    wc,
-    wl,
-    wf,
-    wh,
+    packed,
+    out_ref,
     bias,
-    out_ref,
     tmp,
     rin,
     stem,
@@ -272,6 +288,12 @@
     pooled,
     fin,
 ):
+    wa, wb, wc, wl, wf, wh, ws, wt, wv = parts_of(packed)
+    terms = [
+        jnp.concatenate([wv[32 * k : 32 * k + 16], wv[32 * k + 16 : 32 * k + 32]], axis=1)
+        for k in range(3)
+    ]
+    bias[...] = terms[0].astype(F32) + (terms[1].astype(F32) + terms[2].astype(F32))
     nz, have = r_ref.shape[0:2]
     pitch = tmp.shape[0] // nz
     blocks = cols // 8 + 2
@@ -279,29 +301,42 @@
     leftmost = (pos_ref[0] == 0) & (step == 0)
     rightmost = (pos_ref[0] == parts_gz - 1) & (step == steps - 1)
 
+    def row_of(z):
+        return z % (nz // 8) * 8 + z // (nz // 8)
+
     for z in range(nz):
         tmp[z * pitch : z * pitch + have] = r_ref[z].astype(F32)
     for b in range(blocks):
-        rin[b] = tmp[pl.ds(step * (cols // 8) + b, nz, stride=pitch), :].astype(BF16)
-
-    b_stem = bias[0:1, :]
+        rows = [
+            tmp[pl.ds(step * (cols // 8) + b + k * pitch, 8, stride=nz // 8 * pitch), :]
+            for k in range(nz // 8)
+        ]
+        rin[b] = jnp.concatenate(rows, axis=0).astype(BF16)
+
+    b_stem = bias[0:1, 0:384]
 
     def stem_put(acc, first, i):
         out = relu(acc + b_stem).astype(BF16)
+        low = iota((acc.shape[0], LANES), 1) < 64
+        ends = jnp.where(low, out[:, 0:128], out[:, 128:256])
         for b in range(acc.shape[0] // nz):
-            stem[4 * (first + b) + (i >> 1), i & 1] = out[b * nz : b * nz + nz]
+            at = 4 * (first + b) + (i >> 1)
+            stem[at, i & 1, :, 0:384] = out[b * nz : b * nz + nz]
+            stem[at, i & 1, :, 384:512] = ends[b * nz : b * nz + nz]
+
+    def weight_at(start, depth):
+        return jnp.concatenate([ws[pl.ds(start, depth)], wt[pl.ds(start, depth), 0:128]], axis=1)
 
     def stem_mid(i, carry):
         start = pl.multiple_of(128 - 16 * i, 16)
-        weight = ws[pl.ds(start, LANES), :]
-        stem_put(dot(rin[...].reshape(blocks * nz, LANES), weight), 0, i)
+        stem_put(dot(rin[...].reshape(blocks * nz, LANES), weight_at(start, LANES)), 0, i)
         return carry
 
     lax.fori_loop(1, 7, stem_mid, 0)
     pair = jnp.concatenate([rin[0 : blocks - 1], rin[1:blocks]], axis=-1)
     pair = pair.reshape((blocks - 1) * nz, 2 * LANES)
-    stem_put(dot(pair, ws[0:256]), 1, 0)
-    stem_put(dot(pair, ws[16:272]), 0, 7)
+    stem_put(dot(pair, weight_at(0, 256)), 1, 0)
+    stem_put(dot(pair, weight_at(16, 256)), 0, 7)
 
     @pl.when(leftmost)
     def _():
@@ -312,7 +347,7 @@
         stem[4 * blocks - 4 : 4 * blocks] = jnp.zeros((4,) + stem.shape[1:], BF16)
 
     pairs = cols // 2 + 4
-    mc = divisor(pairs, 512 // nz)
+    mc = divisor(pairs, 1056 // nz)
     m_rows = mc * nz
 
     def skip_step(i, carry):
@@ -322,30 +357,34 @@
             part = stem[pl.ds(m0 + u // 2, mc), u % 2, :, 256 * half : 256 * half + 256]
             return part.reshape(m_rows, 256)
 
-        top = None
+        near = [
+            jnp.concatenate([taken(3 + k, 0), taken(4 + k, 0)], axis=0) for k in range(3)
+        ]
+        acc = dot(jnp.concatenate(near, axis=1), wa[...])
+        acc = relu(acc + bias[1:2, 0:256])
+        best = jnp.maximum(acc[:, 0:128], acc[:, 128:256])
+        top = jnp.maximum(best[0:m_rows], best[m_rows:])
         for p in range(2):
-            acc = dot(taken(3 + p, 0), wa[0:256])
-            acc += dot(taken(4 + p, 0), wa[256:512])
-            acc += dot(taken(5 + p, 0), wa[512:768])
-            acc = relu(acc + bias[1:2, 0:256])
-            skip[pl.ds(m0, mc), p] = acc.astype(BF16).reshape(mc, nz, 256)
-            best = jnp.maximum(acc[:, 0:128], acc[:, 128:256])
-            top = best if top is None else jnp.maximum(top, best)
+            out = acc[p * m_rows : p * m_rows + m_rows].astype(BF16)
+            skip[pl.ds(m0, mc), p] = out.reshape(mc, nz, 256)
         acc = dot(taken(3, 1), wb[0:256])
         for j in range(1, 4):
             acc += dot(taken(3 + j, 1), wb[256 * j : 256 * j + 256])
         best = jnp.maximum(acc[:, 0:128], acc[:, 128:256])
         best = jnp.maximum(best, pltpu.roll(best, 64, axis=1))
         ends = relu(best + bias[2:3, 0:128])
-        z_of = iota((mc, nz, LANES), 1).reshape(m_rows, LANES)
         lane = iota((m_rows, LANES), 1)
-        bottom, summit = z_of == 0, z_of == nz - 1
+        sub = iota((mc, 1, 8, LANES), 2)
 
         def below(x):
-            return jnp.where(bottom, 0.0, pltpu.roll(x, 1, axis=0))
+            x = x.reshape(mc, nz // 8, 8, LANES)
+            turned = jnp.where(sub == 0, 0.0, pltpu.roll(x[:, -1:], 1, axis=2))
+            return jnp.concatenate([turned, x[:, :-1]], axis=1).reshape(m_rows, LANES)
 
         def above(x):
-            return jnp.where(summit, 0.0, pltpu.roll(x, m_rows - 1, axis=0))
+            x = x.reshape(mc, nz // 8, 8, LANES)
+            turned = jnp.where(sub == 7, 0.0, pltpu.roll(x[:, :1], 7, axis=2))
+            return jnp.concatenate([x[:, 1:], turned], axis=1).reshape(m_rows, LANES)
 
         ends_above = above(ends)
         parts = (
@@ -371,7 +410,7 @@
         pooled[pairs - 2 : pairs] = jnp.zeros((2,) + pooled.shape[1:], BF16)
 
     count = cols // 2 + 2
-    nc = divisor(count, 512 // nz)
+    nc = divisor(count, 832 // nz)
     n_rows = nc * nz
 
     def coarse_step(i, carry):
@@ -400,7 +439,7 @@
         stem[cols // 4, 1] = jnp.zeros(stem.shape[2:], BF16)
 
     quads = cols // 4
-    qc = divisor(quads, 512 // nz)
+    qc = divisor(quads, 1024 // nz)
     q_rows = qc * nz
 
     def final_step(i, carry):
@@ -425,7 +464,8 @@
         sides = []
         for side in range(2):
             rows = [
-                fin[side, pl.ds(g * together + k, quads, stride=nz), :] for k in range(together)
+                fin[side, pl.ds(row_of(g * together + k), quads, stride=nz), :]
+                for k in range(together)
             ]
             sides.append(jnp.concatenate(rows, axis=0).astype(BF16))
         h = dot_nt(wh[...], jnp.concatenate(sides, axis=1))
@@ -434,47 +474,48 @@
     size = together * cols
     row = iota((512, size), 0)
     order = jnp.where(iota((512, size), 1) == 4 * (row & 127) + (row >> 7), 1.0, 0.0).astype(BF16)
-    high = table.astype(BF16)
-    rest = table - high.astype(F32)
-    middle = rest.astype(BF16)
-    low = (rest - middle.astype(F32)).astype(BF16)
+    high, middle, low = in_three(table)
     result = dot(high, order) + (dot(middle, order) + dot(low, order))
+    result = result.reshape(groups, 8, size) + bias[8:16, 0:size]
     for g in range(groups):
         for k in range(together):
             for o in range(3):
                 out_ref[o, g * together + k] = (
-                    result[8 * g + 2 * o : 8 * g + 2 * o + 2, k * cols : k * cols + cols]
-                    + b_head[o]
+                    result[g, 2 * o : 2 * o + 2, k * cols : k * cols + cols]
                 )
 
 
-def brick(pos, b_head, received, weights, parts_gz, brick_y, brick_x):
+def brick(pos, received, weights, parts_gz, brick_y, brick_x):
     nz, have = received.shape[0:2]
     cols = brick_x
     while cols * nz > 16384 and cols % 256 == 0:
         cols //= 2
     steps = brick_x // cols
+    scratch = [
+        ((16, 512), F32),
+        ((nz * round_up(have, 8), LANES), F32),
+        ((cols // 8 + 2, nz, LANES), BF16),
+        ((cols // 2 + 8, 2, nz, 512), BF16),
+        ((cols // 2 + 4, 2, nz, 256), BF16),
+        ((cols // 2 + 4, nz, 512), BF16),
+        ((2, cols // 4 * nz, LANES), F32),
+    ]
+    operands = [(received.shape, BF16), (weights.shape, BF16), ((6, nz, 8, cols), F32)]
+    held = sum(math.prod(shape) * jnp.dtype(dtype).itemsize for shape, dtype in scratch + operands)
     vmem = pl.BlockSpec(memory_space=pltpu.VMEM)
     smem = pl.BlockSpec(memory_space=pltpu.SMEM)
     return pl.pallas_call(
         functools.partial(brick_kernel, parts_gz, cols, steps),
         grid=(steps,),
         out_shape=jax.ShapeDtypeStruct((3, nz, brick_y, brick_x), F32),
-        in_specs=[smem, smem] + [vmem] * 9,
+        in_specs=[smem, vmem, vmem],
         out_specs=pl.BlockSpec((3, nz, brick_y, cols), lambda i: (0, 0, 0, i)),
-        scratch_shapes=[
-            pltpu.VMEM((nz * round_up(have, 8), LANES), F32),
-            pltpu.VMEM((cols // 8 + 2, nz, LANES), BF16),
-            pltpu.VMEM((cols // 2 + 8, 2, nz, 512), BF16),
-            pltpu.VMEM((cols // 2 + 4, 2, nz, 256), BF16),
-            pltpu.VMEM((cols // 2 + 4, nz, 512), BF16),
-            pltpu.VMEM((2, cols // 4 * nz, LANES), F32),
-        ],
+        scratch_shapes=[pltpu.VMEM(shape, dtype) for shape, dtype in scratch],
         cost_estimate=pl.CostEstimate(
             flops=20_000_000_000, bytes_accessed=4_000_000, transcendentals=0
         ),
-        compiler_params=pltpu.CompilerParams(vmem_limit_bytes=VMEM_BYTES),
-    )(pos, b_head, received, *weights)
+        compiler_params=pltpu.CompilerParams(vmem_limit_bytes=min(held + 6 * MIB, 60 * MIB)),
+    )(pos, received, weights)
 
 
 def local(
@@ -503,6 +544,7 @@
     b4 = jnp.stack([b_stem, b_skip, b_lift, b_final])
     weights = prepare(
         pos,
+        b_head,
         brick_y,
         full_y,
         w_stem.reshape(w_stem.shape[0:2]),
@@ -514,7 +556,7 @@
         b4,
         b_coarse[None],
     )
-    return brick(pos, b_head, received, weights, parts_gz, brick_y, brick_x)
+    return brick(pos, received, weights, parts_gz, brick_y, brick_x)
 
 
 def solution(mesh):

time: 48.7 us -> 43.9 us (0.901)
  Pallas kernels: 31.8 us -> 25.5 us
  local copies, waits for them, and re-layouts: 2.38 us -> 6.31 us
  waiting for transfers between devices: 5.73 us -> 3.31 us
    pallas_call x1, Pallas kernels: 26.2 us -> 21.9 us  [brick(): pl.pallas_call(functools.partial(brick_kernel, parts_gz, cols, steps), gr...]
    unnamed x13 -> x15, local copies, waits for them, and re-layouts: 2.38 us -> 6.31 us
    all_to_all x1, waiting for transfers between devices: 5.73 us -> 3.31 us  [local(): received = lax.all_to_all(windows, ('gz', 'gy'), 0, 0, tiled=True)]
    pallas_call x1, Pallas kernels: 3.55 us -> 1.69 us  [prepare(): pl.pallas_call(functools.partial(prep_kernel, brick_y, full_y), out_shape...]
    another operation x1, other arithmetic: 0.59 us -> 0.08 us  [local(): pos = jnp.stack([lax.axis_index('gz'), lax.axis_index('gy')]).astype(I32)]
  transfers between devices with their start and end apart: 1 -> 1, of which waited for: 1 -> 1; matrix products, arithmetic and copies ran while one was open for 4% -> 5% of each run, Pallas kernels for 7% -> 4%
where the time goes in v1:
time: 43.9 us; the launch traced here: 43.4 us
  Pallas kernels  25.5 us (58%)
  starting transfers between devices  7.41 us (17%)
  local copies, waits for them, and re-layouts  6.31 us (14%)
  waiting for transfers between devices  3.31 us (8%)
  other arithmetic  0.79 us (2%)
    pallas_call x1, Pallas kernels, brick(): pl.pallas_call(functools.partial(brick_kernel, parts_gz, cols, steps), gr...  21.9 us
    all_to_all x1, starting transfers between devices, local(): received = lax.all_to_all(windows, ('gz', 'gy'), 0, 0, tiled=True)  7.41 us
    unnamed x15, local copies, waits for them, and re-layouts  6.31 us
    all_to_all x1, waiting for transfers between devices, local(): received = lax.all_to_all(windows, ('gz', 'gy'), 0, 0, tiled=True)  3.31 us
    pallas_call x1, Pallas kernels, make_windows(): pl.pallas_call(functools.partial(send_kernel, parts_gz, parts_gy, brick_y...  1.99 us
    pallas_call x1, Pallas kernels, prepare(): pl.pallas_call(functools.partial(prep_kernel, brick_y, full_y), out_shape...  1.69 us
  transfers between devices with their start and end apart: 1, of which 1 were waited for; matrix products, arithmetic and copies ran while one was open for 5% of the time, Pallas kernels for 4%

profile of v1, /device:TPU:0, one launch (start us, length us, event | category | flops | bytes accessed | tf_op | source)
XLA Modules:
  0.0 43.4 jit_solution(9224845000172360870)
XLA Ops:
  0.0 2.0 %shard_map.136 = bf16[32,34,128]{2,1,0:T(8,128)(2,1)} custom-call(s32[1,2]{1,0:T(1,128)} %off_ref.1, bf16[1,16,1024]{2,1,0:T(8,128)(2,1)} %image_ref.1), custom_call_target="tpu_custom_call" | custom-call | tf_op jit(solution)/shard_map/pallas_call | solution.py:87
  2.0 7.4 %all-to-all-start = ((bf16[32,34,128]{2,1,0:T(8,128)(2,1)}), bf16[32,34,128]{2,1,0:T(8,128)(2,1)}, u32[]{:S(2)}, u32[]{:S(2)}) async-start(bf16[32,34,128]{2,1,0:T(8,128)(2,1)} %shard_map.136), calls=%async_computation | async-start | bytes 655360 | tf_op jit(solution)/shard_map/all_to_all | solution.py:543
  9.4 1.2 %copy.15.w_coarse = bf16[27,64,32]{2,1,0:T(8,128)(2,1)S(1)} copy(bf16[27,64,32]{1,2,0:T(8,128)(2,1)} %param.20) | data formatting | bytes 221184 | tf_op args[6]
  10.6 0.1 pad_add_fusion.pos_ref
  10.7 0.7 %pad_maximum_fusion.b4 = f32[4,32]{1,0:T(4,128)S(1)} fusion(f32[1,32]{1,0:T(1,128)} %bitcast.10, f32[1,32]{1,0:T(1,128)} %bitcast.11, f32[1,32]{1,0:T(1,128)} %bitcast.12, f32[1,32]{1,0:T(1,128)} %bitcast.13), kind=kLoop, calls=%fused_computation | loop fusion | flops 384 | bytes 1024 | tf_op jit(solution)/shard_map/stack | solution.py:544
  11.4 0.0 copy-start
  11.4 0.9 %copy-done = bf16[9,32,32]{2,1,0:T(8,128)(2,1)S(1)} copy-done((bf16[9,32,32]{2,1,0:T(8,128)(2,1)S(1)}, bf16[9,32,32]{2,1,0:T(8,128)(2,1)}, u32[]{:S(2)}) %copy-start) | copy-done | bytes 18456
  12.3 0.0 copy-start.1
  12.3 0.9 %copy-done.1 = bf16[9,32,32]{2,1,0:T(8,128)(2,1)S(1)} copy-done((bf16[9,32,32]{2,1,0:T(8,128)(2,1)S(1)}, bf16[9,32,32]{2,1,0:T(8,128)(2,1)}, u32[]{:S(2)}) %copy-start.1) | copy-done | bytes 18456
  13.2 0.0 copy-start.2
  13.2 0.7 %copy-done.2 = bf16[32,64]{1,0:T(8,128)(2,1)S(1)} copy-done((bf16[32,64]{1,0:T(8,128)(2,1)S(1)}, bf16[32,64]{1,0:T(8,128)(2,1)}, u32[]{:S(2)}) %copy-start.2) | copy-done | bytes 4120
  13.9 0.0 copy-start.3
  13.9 0.7 %copy-done.3 = bf16[9,32,1]{1,0,2:T(8,128)(2,1)S(1)} copy-done((bf16[9,32,1]{1,0,2:T(8,128)(2,1)S(1)}, bf16[9,32,1]{1,0,2:T(8,128)(2,1)}, u32[]{:S(2)}) %copy-start.3) | copy-done | bytes 600
  14.5 0.0 copy-start.4
  14.5 0.7 %copy-done.4 = bf16[3,32]{1,0:T(4,128)(2,1)S(1)} copy-done((bf16[3,32]{1,0:T(4,128)(2,1)S(1)}, bf16[3,32]{1,0:T(4,128)(2,1)}, u32[]{:S(2)}) %copy-start.4) | copy-done | bytes 216
  15.2 0.0 copy-start.5
  15.2 0.7 %copy-done.5 = f32[3]{0:T(128)S(1)} copy-done((f32[3]{0:T(128)S(1)}, f32[3]{0:T(128)}, u32[]{:S(2)}) %copy-start.5) | copy-done | bytes 36
  15.9 0.0 copy-start.6
  15.9 0.7 %copy-done.6 = f32[64]{0:T(128)S(1)} copy-done((f32[64]{0:T(128)S(1)}, f32[64]{0:T(128)}, u32[]{:S(2)}) %copy-start.6) | copy-done | bytes 280
  16.5 1.7 %shard_map.137.packed = bf16[5792,256]{1,0:T(8,128)(2,1)S(1)} custom-call(s32[2]{0:T(128)S(1)} %pad_add_fusion.pos_ref, f32[3]{0:T(128)S(1)} %copy-done.5, bf16[9,32]{1,0:T(8,128)(2,1)S(1)} %bitcast.8, bf16[9,32,32]{2,1,0:T(8,128)(2,1)S(1)} %copy-done, bf16[27,64,32]{2,1,0:T(8,128)(2,1)S(1)} %copy.15.w_coarse, bf16[32,64]{1,0:T(8,128)(2,1)S(1)} %copy-done.2, ...), custom_call_target="tpu_custom_call" | custom-call | flops 100000000 | bytes 4000000 | tf_op jit(solution)/shard_map/pallas_call | solution.py:262
  18.2 3.3 %all-to-all-done.r_ref = bf16[32,34,128]{2,1,0:T(8,128)(2,1)} async-done(((bf16[32,34,128]{2,1,0:T(8,128)(2,1)}), bf16[32,34,128]{2,1,0:T(8,128)(2,1)}, u32[]{:S(2)}, u32[]{:S(2)}) %all-to-all-start) | async-done | bytes 278560 | tf_op jit(solution)/shard_map/all_to_all | solution.py:543
  21.5 21.9 %shard_map.138 = f32[3,32,2,256]{3,2,1,0:T(2,128)} custom-call(s32[2]{0:T(128)S(1)} %pad_add_fusion.pos_ref, bf16[32,34,128]{2,1,0:T(8,128)(2,1)} %all-to-all-done.r_ref, bf16[5792,256]{1,0:T(8,128)(2,1)S(1)} %shard_map.137.packed), custom_call_target="tpu_custom_call" | custom-call | flops 20000000000 | bytes 4000000 | tf_op jit(solution)/shard_map/pallas_call | solution.py:507
Async XLA Ops:
  2.0 19.5 %all-to-all-start = ((bf16[32,34,128]{2,1,0:T(8,128)(2,1)}), bf16[32,34,128]{2,1,0:T(8,128)(2,1)}, u32[]{:S(2)}, u32[]{:S(2)}) async-start(bf16[32,34,128]{2,1,0:T(8,128)(2,1)} %shard_map.136), calls=%async_computation | async-start | bytes 655360 | tf_op jit(solution)/shard_map/all_to_all | solution.py:543
  11.4 0.9 %copy-start = (bf16[9,32,32]{2,1,0:T(8,128)(2,1)S(1)}, bf16[9,32,32]{2,1,0:T(8,128)(2,1)}, u32[]{:S(2)}) copy-start(bf16[9,32,32]{2,1,0:T(8,128)(2,1)} %w_skip.1) | copy-start | bytes 55300
  12.3 0.9 %copy-start.1 = (bf16[9,32,32]{2,1,0:T(8,128)(2,1)S(1)}, bf16[9,32,32]{2,1,0:T(8,128)(2,1)}, u32[]{:S(2)}) copy-start(bf16[9,32,32]{2,1,0:T(8,128)(2,1)} %w_final.1) | copy-start | bytes 55300
  13.2 0.7 %copy-start.2 = (bf16[32,64]{1,0:T(8,128)(2,1)S(1)}, bf16[32,64]{1,0:T(8,128)(2,1)}, u32[]{:S(2)}) copy-start(bf16[32,64]{1,0:T(8,128)(2,1)} %w_lift.1) | copy-start | bytes 12292
  13.9 0.7 %copy-start.3 = (bf16[9,32,1]{1,0,2:T(8,128)(2,1)S(1)}, bf16[9,32,1]{1,0,2:T(8,128)(2,1)}, u32[]{:S(2)}) copy-start(bf16[9,32,1]{1,0,2:T(8,128)(2,1)} %param.16) | copy-start | bytes 1732
  14.5 0.7 %copy-start.4 = (bf16[3,32]{1,0:T(4,128)(2,1)S(1)}, bf16[3,32]{1,0:T(4,128)(2,1)}, u32[]{:S(2)}) copy-start(bf16[3,32]{1,0:T(4,128)(2,1)} %w_head.1) | copy-start | bytes 580
  15.2 0.7 %copy-start.5 = (f32[3]{0:T(128)S(1)}, f32[3]{0:T(128)}, u32[]{:S(2)}) copy-start(f32[3]{0:T(128)} %b_head.1) | copy-start | bytes 40
  15.9 0.7 %copy-start.6 = (f32[64]{0:T(128)S(1)}, f32[64]{0:T(128)}, u32[]{:S(2)}) copy-start(f32[64]{0:T(128)} %param.21) | copy-start | bytes 772

commit v2 on v1

--- a/solution.py
+++ b/solution.py
@@ -9,15 +9,23 @@
 from jax.sharding import PartitionSpec as P
 
 MAXOFF = 32
-HALO = 8
-SLOTS = 16
-HALO_Y = 7
 LANES = 128
-PAD = MAXOFF + HALO
+PAD = MAXOFF + 8
 BF16, F32, I32 = jnp.bfloat16, jnp.float32, jnp.int32
 MIB = 1024 * 1024
 
 
+def packing(brick_x, nz):
+    return (9, 14, 6, 6) if chunk(brick_x, nz) == brick_x else (8, 16, 8, 7)
+
+
+def chunk(brick_x, nz):
+    cols = brick_x
+    while cols * nz > 16384 and cols % 256 == 0:
+        cols //= 2
+    return cols
+
+
 def iota(shape, dim):
     return lax.broadcasted_iota(I32, shape, dim)
 
@@ -46,47 +54,52 @@
     return max(d for d in range(1, count + 1) if count % d == 0 and d <= max(most, 1))
 
 
-def send_kernel(parts_gz, parts_gy, brick_y, brick_x, off_ref, image_ref, send_ref, tall_ref):
+def send_kernel(parts_gz, parts_gy, brick_y, brick_x, pack, off_ref, image_ref, send_ref, tall_ref):
+    count, slots, ahead_x, ahead_y = pack
     full_y, full_x = image_ref.shape[1:]
-    blocks = full_x // 8 + 2
-    rows = round_up(blocks, 8)
-    mine = brick_x // 8 + 2
+    rows = send_ref.shape[1]
     off_y, off_x = off_ref[0, 0], off_ref[0, 1]
     tall_ref[...] = jnp.zeros_like(tall_ref)
     tall_ref[PAD : PAD + full_x, 0:full_y] = image_ref[0].astype(F32).T
-    lane, block = iota((rows, LANES), 1), iota((rows, LANES), 0)
-    in_section = (block >= 1) & (block < blocks - 1)
-    halves = full_y // SLOTS
-    packed = [jnp.zeros((rows, LANES), F32) for _ in range(halves)]
-    for i in range(8):
-        column = tall_ref[pl.ds(PAD - HALO + i - off_x, rows, stride=8), :]
-        for h in range(halves):
-            turn = lax.rem(off_y + (16 * i - 16 * h + 2 * LANES), LANES)
-            turned = pltpu.roll(column, turn, axis=1)
-            packed[h] = jnp.where(((lane >> 4) == i) & in_section, turned, packed[h])
-    slot = lane & 15
-    for gy in range(parts_gy):
-        start = brick_y * gy - HALO_Y
-        window = jnp.zeros((rows, LANES), F32)
-        for h in range(halves):
-            shift = start - 16 * h
-            if -16 < shift < 16:
-                turned = pltpu.roll(packed[h], (-shift) % LANES, axis=1)
-                inside = (slot + shift >= 0) & (slot + shift < 16)
-                window = jnp.where(inside, turned, window)
-        for gz in range(parts_gz):
-            first = gz * (brick_x // 8)
-            send_ref[gz * parts_gy + gy] = window[first : first + mine].astype(BF16)
-
-
-def make_windows(image, offsets, parts_gz, parts_gy):
+    lane = iota((rows, LANES), 1)
+    slot = lane
+    for i in range(1, count):
+        slot = jnp.where(lane >= slots * i, lane - slots * i, slot)
+    block = iota((rows, LANES), 0) * count
+    parts = -(-full_y // slots)
+    for gz in range(parts_gz):
+        packed = [jnp.zeros((rows, LANES), F32) for _ in range(parts)]
+        for i in range(count):
+            x = gz * brick_x - ahead_x + i
+            column = tall_ref[pl.ds(PAD + x - off_x, rows, stride=count), :]
+            here = (lane >= slots * i) & (lane < slots * i + slots)
+            here &= (block >= -x) & (block < full_x - x)
+            for h in range(parts):
+                turn = lax.rem(off_y + (slots * (i - h) + 2 * LANES), LANES)
+                turned = pltpu.roll(column, turn, axis=1)
+                packed[h] = jnp.where(here & (slot < full_y - slots * h), turned, packed[h])
+        for gy in range(parts_gy):
+            window = jnp.zeros((rows, LANES), F32)
+            for h in range(parts):
+                shift = brick_y * gy - ahead_y - slots * h
+                if -slots < shift < slots:
+                    turned = packed[h]
+                    if shift:
+                        turned = pltpu.roll(turned, (-shift) % LANES, axis=1)
+                    inside = (slot + shift >= 0) & (slot + shift < slots)
+                    window = jnp.where(inside, turned, window)
+            send_ref[gz * parts_gy + gy] = window.astype(BF16)
+
+
+def make_windows(image, offsets, parts_gz, parts_gy, nz):
     full_y, full_x = image.shape[1:]
     brick_y, brick_x = full_y // parts_gy, full_x // parts_gz
-    rows = round_up(full_x // 8 + 2, 8)
-    tall = round_up(PAD - HALO + 7 + MAXOFF + 8 * (rows - 1) + 1, 8)
+    pack = packing(brick_x, nz)
+    rows = round_up(-(-(brick_x + 6 + pack[2]) // pack[0]), 8)
+    tall = round_up(PAD + full_x - brick_x + MAXOFF + pack[0] * rows, 8)
     return pl.pallas_call(
-        functools.partial(send_kernel, parts_gz, parts_gy, brick_y, brick_x),
-        out_shape=jax.ShapeDtypeStruct((parts_gz * parts_gy, brick_x // 8 + 2, LANES), BF16),
+        functools.partial(send_kernel, parts_gz, parts_gy, brick_y, brick_x, pack),
+        out_shape=jax.ShapeDtypeStruct((parts_gz * parts_gy, rows, LANES), BF16),
         in_specs=[
             pl.BlockSpec(memory_space=pltpu.SMEM),
             pl.BlockSpec(memory_space=pltpu.VMEM),
@@ -99,8 +112,9 @@
 ENDS = (0, 1, 10, 11, 2, 3, 8, 9)
 
 
-SIZES = {"a": 768, "b": 1024, "c": 1536, "l": 256, "f": 1536, "h": 32, "s": 272, "t": 272, "v": 96}
+SIZES = {"a": 768, "b": 1024, "c": 1536, "l": 256, "f": 1536, "h": 32, "v": 96, "s": 736, "t": 368}
 STARTS = dict(zip(SIZES, [sum(list(SIZES.values())[:k]) for k in range(len(SIZES))]))
+MIDDLE = 96
 WEIGHT_ROWS = sum(SIZES.values())
 
 
@@ -126,6 +140,7 @@
 def prep_kernel(
     brick_y,
     full_y,
+    pack,
     pos_ref,
     b_head,
     w_stem,
@@ -139,7 +154,7 @@
     packed,
     bias,
 ):
-    wa, wb, wc, wl, wf, wh, ws, wt, wv = parts_of(packed)
+    wa, wb, wc, wl, wf, wh, wv, ws, wt = parts_of(packed)
     y0 = pos_ref[1] * brick_y
     zero = jnp.zeros((32, 256), F32)
 
@@ -158,17 +173,36 @@
     rep = dot(w_stem[...], t384)
     lane16 = iota((16, 384), 1)
     t16 = stem_row(lane16 >> 5)
-    tap16 = iota((16, 384), 0) - t16 - 1
+    tap16 = iota((16, 384), 0) - t16
     ok16 = within(y0 - 5 + t16, full_y)
-    ws[...] = jnp.zeros((272, 256), BF16)
-    wt[...] = jnp.zeros((272, 256), BF16)
+    taps = []
     for dx in range(3):
         block = jnp.zeros((16, 384), F32)
         for a in range(3):
             block = jnp.where((tap16 == a) & ok16, rep[3 * a + dx : 3 * a + dx + 1], block)
-        block = block.astype(BF16)
-        ws[112 + 16 * dx : 128 + 16 * dx] = block[:, 0:256]
-        wt[112 + 16 * dx : 128 + 16 * dx, 0:128] = block[:, 256:384]
+        taps.append(block)
+    taps = jnp.concatenate(taps, axis=0).astype(BF16)
+    count, slots, _, ahead_y = pack
+    for part, i in enumerate((0, count - 1, None)):
+        depth = 256 if part < 2 else 224
+        row, column = iota((depth, 48), 0), iota((depth, 48), 1)
+        place = jnp.zeros((depth, 48), F32)
+        for dx in range(3):
+            if part < 2:
+                at = i - 1 + dx
+                start = slots * (at % count) + 128 * (at // count + (i == 0))
+            else:
+                start = MIDDLE + slots * dx
+            near = (column >= 16 * dx) & (column < 16 * dx + 14)
+            here = row == start + ahead_y - 6 + column - 16 * dx
+            place = jnp.where(near & here, 1.0, place)
+        block = dot(place.astype(BF16), taps).astype(BF16)
+        ws[256 * part : 256 * part + depth] = block[:, 0:256]
+        if part < 2:
+            wt[0:256, 128 * part : 128 * part + 128] = block[:, 256:384]
+        else:
+            wt[256:368, 0:128] = block[0:112, 256:384]
+            wt[256:368, 128:256] = block[112:224, 256:384]
     bias[...] = jnp.zeros_like(bias)
     bias[0:1, 0:384] = jnp.where(stem_ok, spread(b4[0:1], t384_f), 0.0)
 
@@ -209,7 +243,7 @@
     slots += [(0, 0), (4, 0), (0, 1), (4, 1)]
     q_of = lane >> 6
     for dx in range(3):
-        reps = [dot_tn(w_coarse[3 * ca + dx], t64) for ca in range(9)]
+        reps = [dot(w_coarse[3 * ca + dx], t64) for ca in range(9)]
         for i, (p, c) in enumerate(slots):
             block = zero
             if p is not None:
@@ -257,10 +291,10 @@
         wv[32 * k + 16 : 32 * k + 32] = term[:, 256:512]
 
 
-def prepare(pos, b_head, brick_y, full_y, w_stem, w_skip, w_coarse, w_lift, w_final, w_head, b4, b_coarse):
+def prepare(pos, b_head, brick_y, full_y, pack, w_stem, w_skip, w_coarse, w_lift, w_final, w_head, b4, b_coarse):
     vmem = pl.BlockSpec(memory_space=pltpu.VMEM)
     return pl.pallas_call(
-        functools.partial(prep_kernel, brick_y, full_y),
+        functools.partial(prep_kernel, brick_y, full_y, pack),
         out_shape=jax.ShapeDtypeStruct((WEIGHT_ROWS, 256), BF16),
         in_specs=[pl.BlockSpec(memory_space=pltpu.SMEM)] * 2 + [vmem] * 8,
         out_specs=vmem,
@@ -276,11 +310,14 @@
     parts_gz,
     cols,
     steps,
+    pack,
     pos_ref,
     r_ref,
     packed,
     out_ref,
     bias,
+    shared,
+    middle,
     tmp,
     rin,
     stem,
@@ -288,7 +325,7 @@
     pooled,
     fin,
 ):
-    wa, wb, wc, wl, wf, wh, ws, wt, wv = parts_of(packed)
+    wa, wb, wc, wl, wf, wh, wv, ws, wt = parts_of(packed)
     terms = [
         jnp.concatenate([wv[32 * k : 32 * k + 16], wv[32 * k + 16 : 32 * k + 32]], axis=1)
         for k in range(3)
@@ -296,7 +333,8 @@
     bias[...] = terms[0].astype(F32) + (terms[1].astype(F32) + terms[2].astype(F32))
     nz, have = r_ref.shape[0:2]
     pitch = tmp.shape[0] // nz
-    blocks = cols // 8 + 2
+    per, slots, ahead_x, _ = pack
+    blocks = -(-(cols + 6 + ahead_x) // per)
     step = 0 if steps == 1 else pl.program_id(0)
     leftmost = (pos_ref[0] == 0) & (step == 0)
     rightmost = (pos_ref[0] == parts_gz - 1) & (step == steps - 1)
@@ -320,23 +358,30 @@
         low = iota((acc.shape[0], LANES), 1) < 64
         ends = jnp.where(low, out[:, 0:128], out[:, 128:256])
         for b in range(acc.shape[0] // nz):
-            at = 4 * (first + b) + (i >> 1)
-            stem[at, i & 1, :, 0:384] = out[b * nz : b * nz + nz]
-            stem[at, i & 1, :, 384:512] = ends[b * nz : b * nz + nz]
-
-    def weight_at(start, depth):
-        return jnp.concatenate([ws[pl.ds(start, depth)], wt[pl.ds(start, depth), 0:128]], axis=1)
+            u = per * (first + b) + i + 8 - ahead_x
+            stem[u >> 1, u & 1, :, 0:384] = out[b * nz : b * nz + nz]
+            stem[u >> 1, u & 1, :, 384:512] = ends[b * nz : b * nz + nz]
+
+    shared[:, 0:256] = ws[512:736].astype(F32)
+    shared[0:112, 256:384] = wt[256:368, 0:128].astype(F32)
+    shared[112:224, 256:384] = wt[256:368, 128:256].astype(F32)
+
+    for i in range(per - 2):
+        start = MIDDLE - slots * i
+        middle[i] = shared[start : start + LANES, :].astype(BF16)
 
     def stem_mid(i, carry):
-        start = pl.multiple_of(128 - 16 * i, 16)
-        stem_put(dot(rin[...].reshape(blocks * nz, LANES), weight_at(start, LANES)), 0, i)
+        stem_put(dot(rin[...].reshape(blocks * nz, LANES), middle[i - 1]), 0, i)
         return carry
 
-    lax.fori_loop(1, 7, stem_mid, 0)
+    lax.fori_loop(1, per - 1, stem_mid, 0)
     pair = jnp.concatenate([rin[0 : blocks - 1], rin[1:blocks]], axis=-1)
     pair = pair.reshape((blocks - 1) * nz, 2 * LANES)
-    stem_put(dot(pair, weight_at(0, 256)), 1, 0)
-    stem_put(dot(pair, weight_at(16, 256)), 0, 7)
+    for part, (first, i) in enumerate(((1, 0), (0, per - 1))):
+        weight = jnp.concatenate(
+            [ws[256 * part : 256 * part + 256], wt[0:256, 128 * part : 128 * part + 128]], axis=1
+        )
+        stem_put(dot(pair, weight), first, i)
 
     @pl.when(leftmost)
     def _():
@@ -344,7 +389,7 @@
 
     @pl.when(rightmost)
     def _():
-        stem[4 * blocks - 4 : 4 * blocks] = jnp.zeros((4,) + stem.shape[1:], BF16)
+        stem[cols // 2 + 4 : cols // 2 + 8] = jnp.zeros((4,) + stem.shape[1:], BF16)
 
     pairs = cols // 2 + 4
     mc = divisor(pairs, 1056 // nz)
@@ -487,14 +532,14 @@
 
 def brick(pos, received, weights, parts_gz, brick_y, brick_x):
     nz, have = received.shape[0:2]
-    cols = brick_x
-    while cols * nz > 16384 and cols % 256 == 0:
-        cols //= 2
+    cols, pack = chunk(brick_x, nz), packing(brick_x, nz)
     steps = brick_x // cols
     scratch = [
         ((16, 512), F32),
+        ((224, 384), F32),
+        ((pack[0] - 2, LANES, 384), BF16),
         ((nz * round_up(have, 8), LANES), F32),
-        ((cols // 8 + 2, nz, LANES), BF16),
+        ((-(-(cols + 6 + pack[2]) // pack[0]), nz, LANES), BF16),
         ((cols // 2 + 8, 2, nz, 512), BF16),
         ((cols // 2 + 4, 2, nz, 256), BF16),
         ((cols // 2 + 4, nz, 512), BF16),
@@ -505,7 +550,7 @@
     vmem = pl.BlockSpec(memory_space=pltpu.VMEM)
     smem = pl.BlockSpec(memory_space=pltpu.SMEM)
     return pl.pallas_call(
-        functools.partial(brick_kernel, parts_gz, cols, steps),
+        functools.partial(brick_kernel, parts_gz, cols, steps, pack),
         grid=(steps,),
         out_shape=jax.ShapeDtypeStruct((3, nz, brick_y, brick_x), F32),
         in_specs=[smem, vmem, vmem],
@@ -539,7 +584,8 @@
     brick_y, brick_x = full_y // parts_gy, full_x // parts_gz
     assert image.shape[0] == 1 and brick_y == 2
     pos = jnp.stack([lax.axis_index("gz"), lax.axis_index("gy")]).astype(I32)
-    windows = make_windows(image, offsets, parts_gz, parts_gy)
+    nz = parts_gz * parts_gy
+    windows = make_windows(image, offsets, parts_gz, parts_gy, nz)
     received = lax.all_to_all(windows, ("gz", "gy"), 0, 0, tiled=True)
     b4 = jnp.stack([b_stem, b_skip, b_lift, b_final])
     weights = prepare(
@@ -547,9 +593,10 @@
         b_head,
         brick_y,
         full_y,
+        packing(brick_x, nz),
         w_stem.reshape(w_stem.shape[0:2]),
         w_skip,
-        w_coarse,
+        w_coarse.transpose(0, 2, 1),
         w_lift,
         w_final,
         w_head,

time: 43.9 us -> 42.5 us (0.968)
  waiting for transfers between devices: 3.31 us -> 1.87 us
  Pallas kernels: 25.5 us -> 26 us
    all_to_all x1, waiting for transfers between devices: 3.31 us -> 1.87 us  [local(): received = lax.all_to_all(windows, ('gz', 'gy'), 0, 0, tiled=True)]
    unnamed x15 -> x16, local copies, waits for them, and re-layouts: 6.31 us -> 6.07 us
  transfers between devices with their start and end apart: 1 -> 1, of which waited for: 1 -> 1; matrix products, arithmetic and copies ran while one was open for 5% -> 2% of each run, Pallas kernels for 4% -> 5%
where the time goes in v2:
time: 42.5 us; the launch traced here: 42 us
  Pallas kernels  26 us (61%)
  starting transfers between devices  7.3 us (17%)
  local copies, waits for them, and re-layouts  6.07 us (14%)
  waiting for transfers between devices  1.87 us (4%)
  other arithmetic  0.79 us (2%)
    pallas_call x1, Pallas kernels, brick(): pl.pallas_call(functools.partial(brick_kernel, parts_gz, cols, steps, pac...  21.8 us
    all_to_all x1, starting transfers between devices, local(): received = lax.all_to_all(windows, ('gz', 'gy'), 0, 0, tiled=True)  7.3 us
    unnamed x16, local copies, waits for them, and re-layouts  6.07 us
    pallas_call x1, Pallas kernels, make_windows(): pl.pallas_call(functools.partial(send_kernel, parts_gz, parts_gy, brick_y...  2.3 us
    pallas_call x1, Pallas kernels, prepare(): pl.pallas_call(functools.partial(prep_kernel, brick_y, full_y, pack), out...  1.89 us
    all_to_all x1, waiting for transfers between devices, local(): received = lax.all_to_all(windows, ('gz', 'gy'), 0, 0, tiled=True)  1.87 us
  transfers between devices with their start and end apart: 1, of which 1 were waited for; matrix products, arithmetic and copies ran while one was open for 2% of the time, Pallas kernels for 5%

profile of v2, /device:TPU:0, one launch (start us, length us, event | category | flops | bytes accessed | tf_op | source)
XLA Modules:
  0.0 42.0 jit_solution(18348319359388378927)
XLA Ops:
  0.0 2.3 %shard_map.136 = bf16[32,32,128]{2,1,0:T(8,128)(2,1)} custom-call(s32[1,2]{1,0:T(1,128)} %off_ref.1, bf16[1,16,1024]{2,1,0:T(8,128)(2,1)} %image_ref.1), custom_call_target="tpu_custom_call" | custom-call | tf_op jit(solution)/shard_map/pallas_call | solution.py:100
  2.3 7.3 %all-to-all-start = ((bf16[32,32,128]{2,1,0:T(8,128)(2,1)}), bf16[32,32,128]{2,1,0:T(8,128)(2,1)S(1)}, u32[]{:S(2)}, u32[]{:S(2)}) async-start(bf16[32,32,128]{2,1,0:T(8,128)(2,1)} %shard_map.136), calls=%async_computation | async-start | bytes 524288 | tf_op jit(solution)/shard_map/all_to_all | solution.py:589
  9.6 0.1 pad_add_fusion.pos_ref
  9.7 0.7 %pad_maximum_fusion.b4 = f32[4,32]{1,0:T(4,128)S(1)} fusion(f32[1,32]{1,0:T(1,128)} %bitcast.12, f32[1,32]{1,0:T(1,128)} %bitcast.13, f32[1,32]{1,0:T(1,128)} %bitcast.14, f32[1,32]{1,0:T(1,128)} %bitcast.15), kind=kLoop, calls=%fused_computation | loop fusion | flops 384 | bytes 1024 | tf_op jit(solution)/shard_map/stack | solution.py:590
  10.4 0.0 copy-start
  10.4 0.9 %copy-done = bf16[27,64,32]{1,2,0:T(8,128)(2,1)S(1)} copy-done((bf16[27,64,32]{1,2,0:T(8,128)(2,1)S(1)}, bf16[27,64,32]{1,2,0:T(8,128)(2,1)}, u32[]{:S(2)}) %copy-start) | copy-done | bytes 110616
  11.3 0.0 copy-start.1
  11.3 0.9 %copy-done.1 = bf16[9,32,32]{2,1,0:T(8,128)(2,1)S(1)} copy-done((bf16[9,32,32]{2,1,0:T(8,128)(2,1)S(1)}, bf16[9,32,32]{2,1,0:T(8,128)(2,1)}, u32[]{:S(2)}) %copy-start.1) | copy-done | bytes 18456
  12.2 0.0 copy-start.2
  12.2 0.9 %copy-done.2 = bf16[9,32,32]{2,1,0:T(8,128)(2,1)S(1)} copy-done((bf16[9,32,32]{2,1,0:T(8,128)(2,1)S(1)}, bf16[9,32,32]{2,1,0:T(8,128)(2,1)}, u32[]{:S(2)}) %copy-start.2) | copy-done | bytes 18456
  13.1 0.0 copy-start.3
  13.1 0.7 %copy-done.3 = bf16[32,64]{1,0:T(8,128)(2,1)S(1)} copy-done((bf16[32,64]{1,0:T(8,128)(2,1)S(1)}, bf16[32,64]{1,0:T(8,128)(2,1)}, u32[]{:S(2)}) %copy-start.3) | copy-done | bytes 4120
  13.8 0.0 copy-start.4
  13.8 0.7 %copy-done.4 = bf16[9,32,1]{1,0,2:T(8,128)(2,1)S(1)} copy-done((bf16[9,32,1]{1,0,2:T(8,128)(2,1)S(1)}, bf16[9,32,1]{1,0,2:T(8,128)(2,1)}, u32[]{:S(2)}) %copy-start.4) | copy-done | bytes 600
  14.5 0.0 copy-start.5
  14.5 0.7 %copy-done.5 = bf16[3,32]{1,0:T(4,128)(2,1)S(1)} copy-done((bf16[3,32]{1,0:T(4,128)(2,1)S(1)}, bf16[3,32]{1,0:T(4,128)(2,1)}, u32[]{:S(2)}) %copy-start.5) | copy-done | bytes 216
  15.2 0.0 copy-start.6
  15.2 0.7 %copy-done.6 = f32[3]{0:T(128)S(1)} copy-done((f32[3]{0:T(128)S(1)}, f32[3]{0:T(128)}, u32[]{:S(2)}) %copy-start.6) | copy-done | bytes 36
  15.8 0.0 copy-start.7
  15.8 0.7 %copy-done.7 = f32[64]{0:T(128)S(1)} copy-done((f32[64]{0:T(128)S(1)}, f32[64]{0:T(128)}, u32[]{:S(2)}) %copy-start.7) | copy-done | bytes 280
  16.5 1.9 %shard_map.137.packed = bf16[6352,256]{1,0:T(8,128)(2,1)S(1)} custom-call(s32[2]{0:T(128)S(1)} %pad_add_fusion.pos_ref, f32[3]{0:T(128)S(1)} %copy-done.6, bf16[9,32]{1,0:T(8,128)(2,1)S(1)} %bitcast.10, bf16[9,32,32]{2,1,0:T(8,128)(2,1)S(1)} %copy-done.1, bf16[27,32,64]{2,1,0:T(8,128)(2,1)S(1)} %bitcast.9, bf16[32,64]{1,0:T(8,128)(2,1)S(1)} %copy-done.3, ...), custom_call_target="tpu_custom_call" | custom-call | flops 100000000 | bytes 4000000 | tf_op jit(solution)/shard_map/pallas_call | solution.py:296
  18.4 1.9 %all-to-all-done.r_ref = bf16[32,32,128]{2,1,0:T(8,128)(2,1)S(1)} async-done(((bf16[32,32,128]{2,1,0:T(8,128)(2,1)}), bf16[32,32,128]{2,1,0:T(8,128)(2,1)S(1)}, u32[]{:S(2)}, u32[]{:S(2)}) %all-to-all-start) | async-done | bytes 262176 | tf_op jit(solution)/shard_map/all_to_all | solution.py:589
  20.3 21.8 %shard_map.138 = f32[3,32,2,256]{3,2,1,0:T(2,128)} custom-call(s32[2]{0:T(128)S(1)} %pad_add_fusion.pos_ref, bf16[32,32,128]{2,1,0:T(8,128)(2,1)S(1)} %all-to-all-done.r_ref, bf16[6352,256]{1,0:T(8,128)(2,1)S(1)} %shard_map.137.packed), custom_call_target="tpu_custom_call" | custom-call | flops 20000000000 | bytes 4000000 | tf_op jit(solution)/shard_map/pallas_call | solution.py:552
Async XLA Ops:
  2.3 18.0 %all-to-all-start = ((bf16[32,32,128]{2,1,0:T(8,128)(2,1)}), bf16[32,32,128]{2,1,0:T(8,128)(2,1)S(1)}, u32[]{:S(2)}, u32[]{:S(2)}) async-start(bf16[32,32,128]{2,1,0:T(8,128)(2,1)} %shard_map.136), calls=%async_computation | async-start | bytes 524288 | tf_op jit(solution)/shard_map/all_to_all | solution.py:589
  10.4 0.9 %copy-start = (bf16[27,64,32]{1,2,0:T(8,128)(2,1)S(1)}, bf16[27,64,32]{1,2,0:T(8,128)(2,1)}, u32[]{:S(2)}) copy-start(bf16[27,64,32]{1,2,0:T(8,128)(2,1)} %param.20) | copy-start | bytes 331780
  11.3 0.9 %copy-start.1 = (bf16[9,32,32]{2,1,0:T(8,128)(2,1)S(1)}, bf16[9,32,32]{2,1,0:T(8,128)(2,1)}, u32[]{:S(2)}) copy-start(bf16[9,32,32]{2,1,0:T(8,128)(2,1)} %w_skip.1) | copy-start | bytes 55300
  12.2 0.9 %copy-start.2 = (bf16[9,32,32]{2,1,0:T(8,128)(2,1)S(1)}, bf16[9,32,32]{2,1,0:T(8,128)(2,1)}, u32[]{:S(2)}) copy-start(bf16[9,32,32]{2,1,0:T(8,128)(2,1)} %w_final.1) | copy-start | bytes 55300
  13.1 0.7 %copy-start.3 = (bf16[32,64]{1,0:T(8,128)(2,1)S(1)}, bf16[32,64]{1,0:T(8,128)(2,1)}, u32[]{:S(2)}) copy-start(bf16[32,64]{1,0:T(8,128)(2,1)} %w_lift.1) | copy-start | bytes 12292
  13.8 0.7 %copy-start.4 = (bf16[9,32,1]{1,0,2:T(8,128)(2,1)S(1)}, bf16[9,32,1]{1,0,2:T(8,128)(2,1)}, u32[]{:S(2)}) copy-start(bf16[9,32,1]{1,0,2:T(8,128)(2,1)} %param.16) | copy-start | bytes 1732
  14.5 0.7 %copy-start.5 = (bf16[3,32]{1,0:T(4,128)(2,1)S(1)}, bf16[3,32]{1,0:T(4,128)(2,1)}, u32[]{:S(2)}) copy-start(bf16[3,32]{1,0:T(4,128)(2,1)} %w_head.1) | copy-start | bytes 580
  15.2 0.7 %copy-start.6 = (f32[3]{0:T(128)S(1)}, f32[3]{0:T(128)}, u32[]{:S(2)}) copy-start(f32[3]{0:T(128)} %b_head.1) | copy-start | bytes 40
  15.8 0.7 %copy-start.7 = (f32[64]{0:T(128)S(1)}, f32[64]{0:T(128)}, u32[]{:S(2)}) copy-start(f32[64]{0:T(128)} %param.21) | copy-start | bytes 772

commit v3 on v2

--- a/solution.py
+++ b/solution.py
@@ -374,7 +374,7 @@
         stem_put(dot(rin[...].reshape(blocks * nz, LANES), middle[i - 1]), 0, i)
         return carry
 
-    lax.fori_loop(1, per - 1, stem_mid, 0)
+    lax.fori_loop(1, per - 1, stem_mid, 0, unroll=per - 2)
     pair = jnp.concatenate([rin[0 : blocks - 1], rin[1:blocks]], axis=-1)
     pair = pair.reshape((blocks - 1) * nz, 2 * LANES)
     for part, (first, i) in enumerate(((1, 0), (0, per - 1))):
@@ -392,7 +392,7 @@
         stem[cols // 2 + 4 : cols // 2 + 8] = jnp.zeros((4,) + stem.shape[1:], BF16)
 
     pairs = cols // 2 + 4
-    mc = divisor(pairs, 1056 // nz)
+    mc = divisor(pairs, 2112 // nz)
     m_rows = mc * nz
 
     def skip_step(i, carry):

time: 42.5 us -> 40.9 us (0.962)
  Pallas kernels: 26 us -> 24.4 us
    pallas_call x1, Pallas kernels: 21.8 us -> 20.2 us  [brick(): pl.pallas_call(functools.partial(brick_kernel, parts_gz, cols, steps, pac...]
where the time goes in v3:
time: 40.9 us; the launch traced here: 40.5 us
  Pallas kernels  24.4 us (60%)
  starting transfers between devices  7.3 us (18%)
  local copies, waits for them, and re-layouts  6.07 us (15%)
  waiting for transfers between devices  1.87 us (5%)
  other arithmetic  0.79 us (2%)
    pallas_call x1, Pallas kernels, brick(): pl.pallas_call(functools.partial(brick_kernel, parts_gz, cols, steps, pac...  20.2 us
    all_to_all x1, starting transfers between devices, local(): received = lax.all_to_all(windows, ('gz', 'gy'), 0, 0, tiled=True)  7.3 us
    unnamed x16, local copies, waits for them, and re-layouts  6.07 us
    pallas_call x1, Pallas kernels, make_windows(): pl.pallas_call(functools.partial(send_kernel, parts_gz, parts_gy, brick_y...  2.3 us
    pallas_call x1, Pallas kernels, prepare(): pl.pallas_call(functools.partial(prep_kernel, brick_y, full_y, pack), out...  1.89 us
    all_to_all x1, waiting for transfers between devices, local(): received = lax.all_to_all(windows, ('gz', 'gy'), 0, 0, tiled=True)  1.87 us
  transfers between devices with their start and end apart: 1, of which 1 were waited for; matrix products, arithmetic and copies ran while one was open for 2% of the time, Pallas kernels for 5%

profile of v3, /device:TPU:0, one launch (start us, length us, event | category | flops | bytes accessed | tf_op | source)
XLA Modules:
  0.0 40.5 jit_solution(16007817352987814839)
XLA Ops:
  0.0 2.3 %shard_map.136 = bf16[32,32,128]{2,1,0:T(8,128)(2,1)} custom-call(s32[1,2]{1,0:T(1,128)} %off_ref.1, bf16[1,16,1024]{2,1,0:T(8,128)(2,1)} %image_ref.1), custom_call_target="tpu_custom_call" | custom-call | tf_op jit(solution)/shard_map/pallas_call | solution.py:100
  2.3 7.3 %all-to-all-start = ((bf16[32,32,128]{2,1,0:T(8,128)(2,1)}), bf16[32,32,128]{2,1,0:T(8,128)(2,1)S(1)}, u32[]{:S(2)}, u32[]{:S(2)}) async-start(bf16[32,32,128]{2,1,0:T(8,128)(2,1)} %shard_map.136), calls=%async_computation | async-start | bytes 524288 | tf_op jit(solution)/shard_map/all_to_all | solution.py:589
  9.6 0.1 pad_add_fusion.pos_ref
  9.7 0.7 %pad_maximum_fusion.b4 = f32[4,32]{1,0:T(4,128)S(1)} fusion(f32[1,32]{1,0:T(1,128)} %bitcast.12, f32[1,32]{1,0:T(1,128)} %bitcast.13, f32[1,32]{1,0:T(1,128)} %bitcast.14, f32[1,32]{1,0:T(1,128)} %bitcast.15), kind=kLoop, calls=%fused_computation | loop fusion | flops 384 | bytes 1024 | tf_op jit(solution)/shard_map/stack | solution.py:590
  10.4 0.0 copy-start
  10.4 0.9 %copy-done = bf16[27,64,32]{1,2,0:T(8,128)(2,1)S(1)} copy-done((bf16[27,64,32]{1,2,0:T(8,128)(2,1)S(1)}, bf16[27,64,32]{1,2,0:T(8,128)(2,1)}, u32[]{:S(2)}) %copy-start) | copy-done | bytes 110616
  11.3 0.0 copy-start.1
  11.3 0.9 %copy-done.1 = bf16[9,32,32]{2,1,0:T(8,128)(2,1)S(1)} copy-done((bf16[9,32,32]{2,1,0:T(8,128)(2,1)S(1)}, bf16[9,32,32]{2,1,0:T(8,128)(2,1)}, u32[]{:S(2)}) %copy-start.1) | copy-done | bytes 18456
  12.2 0.0 copy-start.2
  12.2 0.9 %copy-done.2 = bf16[9,32,32]{2,1,0:T(8,128)(2,1)S(1)} copy-done((bf16[9,32,32]{2,1,0:T(8,128)(2,1)S(1)}, bf16[9,32,32]{2,1,0:T(8,128)(2,1)}, u32[]{:S(2)}) %copy-start.2) | copy-done | bytes 18456
  13.1 0.0 copy-start.3
  13.1 0.7 %copy-done.3 = bf16[32,64]{1,0:T(8,128)(2,1)S(1)} copy-done((bf16[32,64]{1,0:T(8,128)(2,1)S(1)}, bf16[32,64]{1,0:T(8,128)(2,1)}, u32[]{:S(2)}) %copy-start.3) | copy-done | bytes 4120
  13.8 0.0 copy-start.4
  13.8 0.7 %copy-done.4 = bf16[9,32,1]{1,0,2:T(8,128)(2,1)S(1)} copy-done((bf16[9,32,1]{1,0,2:T(8,128)(2,1)S(1)}, bf16[9,32,1]{1,0,2:T(8,128)(2,1)}, u32[]{:S(2)}) %copy-start.4) | copy-done | bytes 600
  14.5 0.0 copy-start.5
  14.5 0.7 %copy-done.5 = bf16[3,32]{1,0:T(4,128)(2,1)S(1)} copy-done((bf16[3,32]{1,0:T(4,128)(2,1)S(1)}, bf16[3,32]{1,0:T(4,128)(2,1)}, u32[]{:S(2)}) %copy-start.5) | copy-done | bytes 216
  15.2 0.0 copy-start.6
  15.2 0.7 %copy-done.6 = f32[3]{0:T(128)S(1)} copy-done((f32[3]{0:T(128)S(1)}, f32[3]{0:T(128)}, u32[]{:S(2)}) %copy-start.6) | copy-done | bytes 36
  15.8 0.0 copy-start.7
  15.8 0.7 %copy-done.7 = f32[64]{0:T(128)S(1)} copy-done((f32[64]{0:T(128)S(1)}, f32[64]{0:T(128)}, u32[]{:S(2)}) %copy-start.7) | copy-done | bytes 280
  16.5 1.9 %shard_map.137.packed = bf16[6352,256]{1,0:T(8,128)(2,1)S(1)} custom-call(s32[2]{0:T(128)S(1)} %pad_add_fusion.pos_ref, f32[3]{0:T(128)S(1)} %copy-done.6, bf16[9,32]{1,0:T(8,128)(2,1)S(1)} %bitcast.10, bf16[9,32,32]{2,1,0:T(8,128)(2,1)S(1)} %copy-done.1, bf16[27,32,64]{2,1,0:T(8,128)(2,1)S(1)} %bitcast.9, bf16[32,64]{1,0:T(8,128)(2,1)S(1)} %copy-done.3, ...), custom_call_target="tpu_custom_call" | custom-call | flops 100000000 | bytes 4000000 | tf_op jit(solution)/shard_map/pallas_call | solution.py:296
  18.4 1.9 %all-to-all-done.r_ref = bf16[32,32,128]{2,1,0:T(8,128)(2,1)S(1)} async-done(((bf16[32,32,128]{2,1,0:T(8,128)(2,1)}), bf16[32,32,128]{2,1,0:T(8,128)(2,1)S(1)}, u32[]{:S(2)}, u32[]{:S(2)}) %all-to-all-start) | async-done | bytes 262176 | tf_op jit(solution)/shard_map/all_to_all | solution.py:589
  20.3 20.2 %shard_map.138 = f32[3,32,2,256]{3,2,1,0:T(2,128)} custom-call(s32[2]{0:T(128)S(1)} %pad_add_fusion.pos_ref, bf16[32,32,128]{2,1,0:T(8,128)(2,1)S(1)} %all-to-all-done.r_ref, bf16[6352,256]{1,0:T(8,128)(2,1)S(1)} %shard_map.137.packed), custom_call_target="tpu_custom_call" | custom-call | flops 20000000000 | bytes 4000000 | tf_op jit(solution)/shard_map/pallas_call | solution.py:552
Async XLA Ops:
  2.3 18.0 %all-to-all-start = ((bf16[32,32,128]{2,1,0:T(8,128)(2,1)}), bf16[32,32,128]{2,1,0:T(8,128)(2,1)S(1)}, u32[]{:S(2)}, u32[]{:S(2)}) async-start(bf16[32,32,128]{2,1,0:T(8,128)(2,1)} %shard_map.136), calls=%async_computation | async-start | bytes 524288 | tf_op jit(solution)/shard_map/all_to_all | solution.py:589
  10.4 0.9 %copy-start = (bf16[27,64,32]{1,2,0:T(8,128)(2,1)S(1)}, bf16[27,64,32]{1,2,0:T(8,128)(2,1)}, u32[]{:S(2)}) copy-start(bf16[27,64,32]{1,2,0:T(8,128)(2,1)} %param.20) | copy-start | bytes 331780
  11.3 0.9 %copy-start.1 = (bf16[9,32,32]{2,1,0:T(8,128)(2,1)S(1)}, bf16[9,32,32]{2,1,0:T(8,128)(2,1)}, u32[]{:S(2)}) copy-start(bf16[9,32,32]{2,1,0:T(8,128)(2,1)} %w_skip.1) | copy-start | bytes 55300
  12.2 0.9 %copy-start.2 = (bf16[9,32,32]{2,1,0:T(8,128)(2,1)S(1)}, bf16[9,32,32]{2,1,0:T(8,128)(2,1)}, u32[]{:S(2)}) copy-start(bf16[9,32,32]{2,1,0:T(8,128)(2,1)} %w_final.1) | copy-start | bytes 55300
  13.1 0.7 %copy-start.3 = (bf16[32,64]{1,0:T(8,128)(2,1)S(1)}, bf16[32,64]{1,0:T(8,128)(2,1)}, u32[]{:S(2)}) copy-start(bf16[32,64]{1,0:T(8,128)(2,1)} %w_lift.1) | copy-start | bytes 12292
  13.8 0.7 %copy-start.4 = (bf16[9,32,1]{1,0,2:T(8,128)(2,1)S(1)}, bf16[9,32,1]{1,0,2:T(8,128)(2,1)}, u32[]{:S(2)}) copy-start(bf16[9,32,1]{1,0,2:T(8,128)(2,1)} %param.16) | copy-start | bytes 1732
  14.5 0.7 %copy-start.5 = (bf16[3,32]{1,0:T(4,128)(2,1)S(1)}, bf16[3,32]{1,0:T(4,128)(2,1)}, u32[]{:S(2)}) copy-start(bf16[3,32]{1,0:T(4,128)(2,1)} %w_head.1) | copy-start | bytes 580
  15.2 0.7 %copy-start.6 = (f32[3]{0:T(128)S(1)}, f32[3]{0:T(128)}, u32[]{:S(2)}) copy-start(f32[3]{0:T(128)} %b_head.1) | copy-start | bytes 40
  15.8 0.7 %copy-start.7 = (f32[64]{0:T(128)S(1)}, f32[64]{0:T(128)}, u32[]{:S(2)}) copy-start(f32[64]{0:T(128)} %param.21) | copy-start | bytes 772

commit v4 on v3

--- a/solution.py
+++ b/solution.py
@@ -455,7 +455,7 @@
         pooled[pairs - 2 : pairs] = jnp.zeros((2,) + pooled.shape[1:], BF16)
 
     count = cols // 2 + 2
-    nc = divisor(count, 832 // nz)
+    nc = divisor(count, 2080 // nz)
     n_rows = nc * nz
 
     def coarse_step(i, carry):

time: 40.9 us -> 40.2 us (0.983)
  Pallas kernels: 24.4 us -> 23.7 us
    pallas_call x1, Pallas kernels: 20.2 us -> 19.5 us  [brick(): pl.pallas_call(functools.partial(brick_kernel, parts_gz, cols, steps, pac...]
where the time goes in v4:
time: 40.2 us; the launch traced here: 39.7 us
  Pallas kernels  23.7 us (59%)
  starting transfers between devices  7.3 us (18%)
  local copies, waits for them, and re-layouts  6.07 us (15%)
  waiting for transfers between devices  1.87 us (5%)
  other arithmetic  0.79 us (2%)
    pallas_call x1, Pallas kernels, brick(): pl.pallas_call(functools.partial(brick_kernel, parts_gz, cols, steps, pac...  19.5 us
    all_to_all x1, starting transfers between devices, local(): received = lax.all_to_all(windows, ('gz', 'gy'), 0, 0, tiled=True)  7.3 us
    unnamed x16, local copies, waits for them, and re-layouts  6.07 us
    pallas_call x1, Pallas kernels, make_windows(): pl.pallas_call(functools.partial(send_kernel, parts_gz, parts_gy, brick_y...  2.3 us
    pallas_call x1, Pallas kernels, prepare(): pl.pallas_call(functools.partial(prep_kernel, brick_y, full_y, pack), out...  1.89 us
    all_to_all x1, waiting for transfers between devices, local(): received = lax.all_to_all(windows, ('gz', 'gy'), 0, 0, tiled=True)  1.87 us
  transfers between devices with their start and end apart: 1, of which 1 were waited for; matrix products, arithmetic and copies ran while one was open for 2% of the time, Pallas kernels for 5%

profile of v4, /device:TPU:0, one launch (start us, length us, event | category | flops | bytes accessed | tf_op | source)
XLA Modules:
  0.0 39.7 jit_solution(2846693018946478712)
XLA Ops:
  0.0 2.3 %shard_map.136 = bf16[32,32,128]{2,1,0:T(8,128)(2,1)} custom-call(s32[1,2]{1,0:T(1,128)} %off_ref.1, bf16[1,16,1024]{2,1,0:T(8,128)(2,1)} %image_ref.1), custom_call_target="tpu_custom_call" | custom-call | tf_op jit(solution)/shard_map/pallas_call | solution.py:100
  2.3 7.3 %all-to-all-start = ((bf16[32,32,128]{2,1,0:T(8,128)(2,1)}), bf16[32,32,128]{2,1,0:T(8,128)(2,1)S(1)}, u32[]{:S(2)}, u32[]{:S(2)}) async-start(bf16[32,32,128]{2,1,0:T(8,128)(2,1)} %shard_map.136), calls=%async_computation | async-start | bytes 524288 | tf_op jit(solution)/shard_map/all_to_all | solution.py:589
  9.6 0.1 pad_add_fusion.pos_ref
  9.7 0.7 %pad_maximum_fusion.b4 = f32[4,32]{1,0:T(4,128)S(1)} fusion(f32[1,32]{1,0:T(1,128)} %bitcast.12, f32[1,32]{1,0:T(1,128)} %bitcast.13, f32[1,32]{1,0:T(1,128)} %bitcast.14, f32[1,32]{1,0:T(1,128)} %bitcast.15), kind=kLoop, calls=%fused_computation | loop fusion | flops 384 | bytes 1024 | tf_op jit(solution)/shard_map/stack | solution.py:590
  10.4 0.0 copy-start
  10.4 0.9 %copy-done = bf16[27,64,32]{1,2,0:T(8,128)(2,1)S(1)} copy-done((bf16[27,64,32]{1,2,0:T(8,128)(2,1)S(1)}, bf16[27,64,32]{1,2,0:T(8,128)(2,1)}, u32[]{:S(2)}) %copy-start) | copy-done | bytes 110616
  11.3 0.0 copy-start.1
  11.3 0.9 %copy-done.1 = bf16[9,32,32]{2,1,0:T(8,128)(2,1)S(1)} copy-done((bf16[9,32,32]{2,1,0:T(8,128)(2,1)S(1)}, bf16[9,32,32]{2,1,0:T(8,128)(2,1)}, u32[]{:S(2)}) %copy-start.1) | copy-done | bytes 18456
  12.2 0.0 copy-start.2
  12.2 0.9 %copy-done.2 = bf16[9,32,32]{2,1,0:T(8,128)(2,1)S(1)} copy-done((bf16[9,32,32]{2,1,0:T(8,128)(2,1)S(1)}, bf16[9,32,32]{2,1,0:T(8,128)(2,1)}, u32[]{:S(2)}) %copy-start.2) | copy-done | bytes 18456
  13.1 0.0 copy-start.3
  13.1 0.7 %copy-done.3 = bf16[32,64]{1,0:T(8,128)(2,1)S(1)} copy-done((bf16[32,64]{1,0:T(8,128)(2,1)S(1)}, bf16[32,64]{1,0:T(8,128)(2,1)}, u32[]{:S(2)}) %copy-start.3) | copy-done | bytes 4120
  13.8 0.0 copy-start.4
  13.8 0.7 %copy-done.4 = bf16[9,32,1]{1,0,2:T(8,128)(2,1)S(1)} copy-done((bf16[9,32,1]{1,0,2:T(8,128)(2,1)S(1)}, bf16[9,32,1]{1,0,2:T(8,128)(2,1)}, u32[]{:S(2)}) %copy-start.4) | copy-done | bytes 600
  14.5 0.0 copy-start.5
  14.5 0.7 %copy-done.5 = bf16[3,32]{1,0:T(4,128)(2,1)S(1)} copy-done((bf16[3,32]{1,0:T(4,128)(2,1)S(1)}, bf16[3,32]{1,0:T(4,128)(2,1)}, u32[]{:S(2)}) %copy-start.5) | copy-done | bytes 216
  15.2 0.0 copy-start.6
  15.2 0.7 %copy-done.6 = f32[3]{0:T(128)S(1)} copy-done((f32[3]{0:T(128)S(1)}, f32[3]{0:T(128)}, u32[]{:S(2)}) %copy-start.6) | copy-done | bytes 36
  15.8 0.0 copy-start.7
  15.8 0.7 %copy-done.7 = f32[64]{0:T(128)S(1)} copy-done((f32[64]{0:T(128)S(1)}, f32[64]{0:T(128)}, u32[]{:S(2)}) %copy-start.7) | copy-done | bytes 280
  16.5 1.9 %shard_map.137.packed = bf16[6352,256]{1,0:T(8,128)(2,1)S(1)} custom-call(s32[2]{0:T(128)S(1)} %pad_add_fusion.pos_ref, f32[3]{0:T(128)S(1)} %copy-done.6, bf16[9,32]{1,0:T(8,128)(2,1)S(1)} %bitcast.10, bf16[9,32,32]{2,1,0:T(8,128)(2,1)S(1)} %copy-done.1, bf16[27,32,64]{2,1,0:T(8,128)(2,1)S(1)} %bitcast.9, bf16[32,64]{1,0:T(8,128)(2,1)S(1)} %copy-done.3, ...), custom_call_target="tpu_custom_call" | custom-call | flops 100000000 | bytes 4000000 | tf_op jit(solution)/shard_map/pallas_call | solution.py:296
  18.4 1.9 %all-to-all-done.r_ref = bf16[32,32,128]{2,1,0:T(8,128)(2,1)S(1)} async-done(((bf16[32,32,128]{2,1,0:T(8,128)(2,1)}), bf16[32,32,128]{2,1,0:T(8,128)(2,1)S(1)}, u32[]{:S(2)}, u32[]{:S(2)}) %all-to-all-start) | async-done | bytes 262176 | tf_op jit(solution)/shard_map/all_to_all | solution.py:589
  20.3 19.5 %shard_map.138 = f32[3,32,2,256]{3,2,1,0:T(2,128)} custom-call(s32[2]{0:T(128)S(1)} %pad_add_fusion.pos_ref, bf16[32,32,128]{2,1,0:T(8,128)(2,1)S(1)} %all-to-all-done.r_ref, bf16[6352,256]{1,0:T(8,128)(2,1)S(1)} %shard_map.137.packed), custom_call_target="tpu_custom_call" | custom-call | flops 20000000000 | bytes 4000000 | tf_op jit(solution)/shard_map/pallas_call | solution.py:552
Async XLA Ops:
  2.3 18.0 %all-to-all-start = ((bf16[32,32,128]{2,1,0:T(8,128)(2,1)}), bf16[32,32,128]{2,1,0:T(8,128)(2,1)S(1)}, u32[]{:S(2)}, u32[]{:S(2)}) async-start(bf16[32,32,128]{2,1,0:T(8,128)(2,1)} %shard_map.136), calls=%async_computation | async-start | bytes 524288 | tf_op jit(solution)/shard_map/all_to_all | solution.py:589
  10.4 0.9 %copy-start = (bf16[27,64,32]{1,2,0:T(8,128)(2,1)S(1)}, bf16[27,64,32]{1,2,0:T(8,128)(2,1)}, u32[]{:S(2)}) copy-start(bf16[27,64,32]{1,2,0:T(8,128)(2,1)} %param.20) | copy-start | bytes 331780
  11.3 0.9 %copy-start.1 = (bf16[9,32,32]{2,1,0:T(8,128)(2,1)S(1)}, bf16[9,32,32]{2,1,0:T(8,128)(2,1)}, u32[]{:S(2)}) copy-start(bf16[9,32,32]{2,1,0:T(8,128)(2,1)} %w_skip.1) | copy-start | bytes 55300
  12.2 0.9 %copy-start.2 = (bf16[9,32,32]{2,1,0:T(8,128)(2,1)S(1)}, bf16[9,32,32]{2,1,0:T(8,128)(2,1)}, u32[]{:S(2)}) copy-start(bf16[9,32,32]{2,1,0:T(8,128)(2,1)} %w_final.1) | copy-start | bytes 55300
  13.1 0.7 %copy-start.3 = (bf16[32,64]{1,0:T(8,128)(2,1)S(1)}, bf16[32,64]{1,0:T(8,128)(2,1)}, u32[]{:S(2)}) copy-start(bf16[32,64]{1,0:T(8,128)(2,1)} %w_lift.1) | copy-start | bytes 12292
  13.8 0.7 %copy-start.4 = (bf16[9,32,1]{1,0,2:T(8,128)(2,1)S(1)}, bf16[9,32,1]{1,0,2:T(8,128)(2,1)}, u32[]{:S(2)}) copy-start(bf16[9,32,1]{1,0,2:T(8,128)(2,1)} %param.16) | copy-start | bytes 1732
  14.5 0.7 %copy-start.5 = (bf16[3,32]{1,0:T(4,128)(2,1)S(1)}, bf16[3,32]{1,0:T(4,128)(2,1)}, u32[]{:S(2)}) copy-start(bf16[3,32]{1,0:T(4,128)(2,1)} %w_head.1) | copy-start | bytes 580
  15.2 0.7 %copy-start.6 = (f32[3]{0:T(128)S(1)}, f32[3]{0:T(128)}, u32[]{:S(2)}) copy-start(f32[3]{0:T(128)} %b_head.1) | copy-start | bytes 40
  15.8 0.7 %copy-start.7 = (f32[64]{0:T(128)S(1)}, f32[64]{0:T(128)}, u32[]{:S(2)}) copy-start(f32[64]{0:T(128)} %param.21) | copy-start | bytes 772
